TPU v7x, 512 devices: a whole 4x4x16 slice. The times are simulated.
512 devices in a mesh: row: 32 (over z_lo, y), col: 16 (over z_hi, x, core).
Axes of the slice: x: 4, y: 4, z: 16 (z_hi: 2, z_lo: 8; z = z_hi * 8 + z_lo), core: 2. Of those that a mesh axis runs over, the one named last changes fastest.
Arguments:
- entries: int32 [128, 64, 128, 128], P('row', 'col'), may hold values from -2 to 2
- tile_cols: int32 [128, 64], P('row', 'col'), may hold values from 0 to 31
- block_now: int32 [32, 65536], P(None, ('col', 'row')), may hold values from 0 to 65520
- block_prev: int32 [32, 65536], P(None, ('col', 'row')), may hold values from 0 to 65520
- block_prev2: int32 [32, 65536], P(None, ('col', 'row')), may hold values from 0 to 65520
- gram_prev: int32 [32, 32], replicated, may hold values from 0 to 65520
- square_prev: int32 [32, 32], replicated, may hold values from 0 to 65520
- inverse_prev: int32 [32, 32], replicated, may hold values from 0 to 65520
- inverse_prev2: int32 [32, 32], replicated, may hold values from 0 to 65520
Outputs:
- next_block: float32 [32, 65536], P(None, ('col', 'row'))
- later_block: float32 [32, 65536], P(None, ('col', 'row'))
Inputs may be any that keep to these rules, and one draw needn't show every extreme that they name: `tile_cols`: stored tiles that name the same tile column in one tile row add. `block_prev`: residues. `block_prev2`: residues. `gram_prev`: residues. `square_prev`: residues. `inverse_prev`: residues. `inverse_prev2`: residues.
All inputs are finite; a program needn't handle non-finite values.
Results may differ from a plain program's by a relative error of at most 0.0003.
Values sent between devices are 32-bit elements; how exact they have to be, the bound alone decides.
No kernel may reach another device: no remote copies, remote signals or barrier semaphores. Data moves between devices by JAX's collectives and lax.ppermute only.
A program may use at most 64 MiB of HBM per device.

v0:
```python
import jax
import jax.numpy as jnp
from jax import lax
from jax.sharding import PartitionSpec as P

modulus = 65521.0


def residue(values):
    return jnp.mod(values, modulus)


def split_digits(values):
    top_part = jnp.floor(values / 256.0)
    return (top_part, values - top_part * 256.0)


def fold_digits(top_sum, low_sum):
    return residue(residue(residue(top_sum) * 256.0) + residue(low_sum))


def fold_three(upper_part, middle, lower_part):
    return residue(
        residue(residue(upper_part) * 15.0) + residue(residue(middle) * 256.0) + residue(lower_part)
    )


def mulmod(left_side, right_side):
    top_part, low_part = split_digits(right_side)
    return fold_digits(left_side * top_part, left_side * low_part)


def exact_dot(left_side, right_side):
    return jnp.dot(
        left_side, right_side, precision=lax.Precision.HIGHEST, preferred_element_type=jnp.float32
    )


def small_product(left_side, right_side):
    left_top, left_low = split_digits(left_side)
    right_top, right_low = split_digits(right_side)
    return fold_three(
        exact_dot(left_top, right_top),
        exact_dot(left_top, right_low) + exact_dot(left_low, right_top),
        exact_dot(left_low, right_low),
    )


def inverse_scalar(number):
    result = jnp.ones_like(number)
    square = number
    exponent = 65519
    for position in range(16):
        if exponent >> position & 1:
            result = mulmod(result, square)
        square = mulmod(square, square)
    return result


def inverse_matrix(matrix):
    matrix_order = matrix.shape[0]
    augmented = jnp.concatenate([matrix, jnp.eye(matrix_order, dtype=matrix.dtype)], axis=1)
    row_numbers = jnp.arange(matrix_order, dtype=jnp.int32)

    def eliminate(column, augmented):
        column = jnp.asarray(column).astype(jnp.int32)
        pivot_column = augmented[:, column]
        usable = (pivot_column != 0.0) & (row_numbers >= column)
        pivot_row_id = jnp.where(jnp.any(usable), jnp.argmax(usable), column)
        pivot_row = augmented[pivot_row_id]
        current_row = augmented[column]
        swapped = jnp.where(
            (row_numbers == column)[:, None],
            pivot_row[None, :],
            jnp.where((row_numbers == pivot_row_id)[:, None], current_row[None, :], augmented),
        )
        scaled = mulmod(pivot_row, inverse_scalar(pivot_row[column]))
        factors = jnp.where(row_numbers == column, 0.0, swapped[:, column])
        reduced = residue(swapped - mulmod(factors[:, None], scaled[None, :]) + modulus)
        return jnp.where((row_numbers == column)[:, None], scaled[None, :], reduced)

    augmented = lax.fori_loop(0, matrix_order, eliminate, augmented)
    return augmented[:, matrix_order:]


def coefficients(
    gram_now, square_now, inverse_now, inverse_prev, inverse_prev2, gram_old, square_old
):
    identity = jnp.eye(gram_now.shape[0], dtype=gram_now.dtype)
    first = residue(identity - small_product(residue(square_now + gram_now), inverse_now) + modulus)
    second = residue(modulus - small_product(gram_now, inverse_prev))
    middle = residue(identity - small_product(inverse_prev, gram_old) + modulus)
    third = residue(
        modulus
        - small_product(small_product(residue(square_old + gram_old), middle), inverse_prev2)
    )
    return jnp.concatenate([first, second, third], axis=1)


def digit_stack(values):
    top_part, low_part = split_digits(values)
    return jnp.stack([top_part, low_part]).astype(jnp.bfloat16)


def combine_blocks(coeffs, stacked):
    products = jnp.einsum(
        "dab,ebn->dean",
        digit_stack(coeffs),
        digit_stack(stacked),
        preferred_element_type=jnp.float32,
    )
    return fold_three(products[0, 0], products[0, 1] + products[1, 0], products[1, 1])


def gram_local(first, second):
    column_count = first.shape[1]
    group_width = min(column_count, 128)
    groups = column_count // group_width
    first_digits = digit_stack(first).reshape(2, first.shape[0], groups, group_width)
    second_digits = digit_stack(second).reshape(2, second.shape[0], groups, group_width)
    products = jnp.einsum(
        "dagw,ecgw->gdeac", first_digits, second_digits, preferred_element_type=jnp.float32
    )
    per_group = fold_three(
        products[:, 0, 0], products[:, 0, 1] + products[:, 1, 0], products[:, 1, 1]
    )
    return residue(jnp.sum(per_group, axis=0))


def digit_pair(values):
    top_part, low_part = split_digits(values)
    return jnp.stack([top_part, low_part])


def forward_partial(block_full, tile_values, tile_cols):
    tile_rows, slot_count, tile_size = (
        tile_values.shape[0],
        tile_values.shape[1],
        tile_values.shape[2],
    )
    block_rows = block_full.shape[0]
    top_part, low_part = split_digits(block_full)
    digits = jnp.concatenate([top_part, low_part], axis=0).astype(jnp.bfloat16)
    digits = digits.reshape(2 * block_rows, -1, tile_size)
    picked = jnp.take(digits, tile_cols.reshape(-1), axis=1).reshape(
        2 * block_rows, tile_rows, slot_count, tile_size
    )
    raw_sums = jnp.einsum("brsk,rsjk->brj", picked, tile_values, preferred_element_type=jnp.float32)
    return fold_digits(raw_sums[:block_rows], raw_sums[block_rows:]).reshape(
        block_rows, tile_rows * tile_size
    )


def backward_partial(projected, tile_values, onehot):
    tile_rows, tile_size = (tile_values.shape[0], tile_values.shape[2])
    block_rows = projected.shape[0]
    top_part, low_part = split_digits(projected)
    digits = (
        jnp.concatenate([top_part, low_part], axis=0)
        .astype(jnp.bfloat16)
        .reshape(2 * block_rows, tile_rows, tile_size)
    )
    spread = jnp.einsum("brj,rsjk->brsk", digits, tile_values, preferred_element_type=jnp.float32)
    raw_sums = jnp.einsum(
        "brsk,rsc->bck",
        spread,
        onehot,
        precision=lax.Precision.HIGHEST,
        preferred_element_type=jnp.float32,
    )
    return fold_digits(raw_sums[:block_rows], raw_sums[block_rows:]).reshape(block_rows, -1)


def body(
    entries,
    tile_cols,
    block_now,
    block_prev,
    block_prev2,
    gram_prev,
    square_prev,
    inverse_prev,
    inverse_prev2,
):
    tile_values = entries.astype(jnp.bfloat16)
    tile_size = tile_values.shape[2]
    share_width = block_now.shape[1]
    col_tiles = share_width * lax.axis_size("row") // tile_size
    onehot = (
        tile_cols[:, :, None] == jnp.arange(col_tiles, dtype=jnp.int32)[None, None, :]
    ).astype(jnp.float32)
    current = block_now.astype(jnp.float32)
    earlier = block_prev.astype(jnp.float32)
    earliest = block_prev2.astype(jnp.float32)
    gram_old = gram_prev.astype(jnp.float32)
    square_old = square_prev.astype(jnp.float32)
    inverse_old = inverse_prev.astype(jnp.float32)
    inverse_older = inverse_prev2.astype(jnp.float32)
    results = []
    for iteration in range(2):
        block_full = lax.all_gather(current, "row", axis=1, tiled=True)
        projected = residue(lax.psum(forward_partial(block_full, tile_values, tile_cols), "col"))
        partial_term = backward_partial(projected, tile_values, onehot)
        applied = residue(lax.psum_scatter(partial_term, "row", scatter_dimension=1, tiled=True))
        current_own = current
        both_sums = lax.psum(
            jnp.stack(
                [
                    digit_pair(gram_local(current_own, applied)),
                    digit_pair(gram_local(applied, applied)),
                ]
            ),
            ("row", "col"),
        )
        gram_now = fold_digits(both_sums[0, 0], both_sums[0, 1])
        square_now = fold_digits(both_sums[1, 0], both_sums[1, 1])
        inverse_now = inverse_matrix(gram_now)
        coeffs = coefficients(
            gram_now, square_now, inverse_now, inverse_old, inverse_older, gram_old, square_old
        )
        stacked = jnp.concatenate([current, earlier, earliest], axis=0)
        following = residue(applied + combine_blocks(coeffs, stacked))
        results.append(following / modulus)
        earliest, earlier, current = (earlier, current, following)
        inverse_older, inverse_old = (inverse_old, inverse_now)
        gram_old, square_old = (gram_now, square_now)
    return (results[0], results[1])


def solution(mesh):
    placed = (
        P("row", "col", None, None),
        P("row", "col"),
        P(None, ("col", "row")),
        P(None, ("col", "row")),
        P(None, ("col", "row")),
        P(),
        P(),
        P(),
        P(),
    )
    return jax.shard_map(
        body,
        mesh=mesh,
        in_specs=placed,
        out_specs=(P(None, ("col", "row")), P(None, ("col", "row"))),
        check_vma=False,
    )
```

profile of v0, /device:TPU:1, one launch (start us, length us, event | category | flops | bytes accessed | tf_op | source)
XLA Modules:
  0.0 2244.6 jit_solution(948067549384732013)
XLA Ops:
  7.2 0.8 reshape.1652
  8.8 114.7 %all_gather.6 = f32[32,4096]{1,0:T(8,128)S(1)} all-gather(f32[32,128]{1,0:T(8,128)S(1)} %get-tuple-element.319), channel_id=1, replica_groups=mesh['row'=32,'col'=16] {'row'}, dimensions={1}, use_global_device_ids=true | all-gather | bytes 540672 | tf_op jit(solution)/shard_map/all_gather | solution.py:201
  124.9 0.8 copy_bitcast_fusion.7
  129.3 247.2 %all-reduce.3.cloned.1.call-done = f32[32,512]{1,0:T(8,128)} async-done(((f32[32,512]{1,0:T(8,128)}), f32[32,512]{1,0:T(8,128)}) %all-reduce.3.cloned.1.call-update) | async-done | bytes 65552 | tf_op jit(solution)/shard_map/psum | solution.py:202
  376.5 0.9 fusion.102
  378.1 1.1 convolution_bitcast_fusion.1
  379.2 1.1 add_select_fusion.22
  380.3 1.1 copy.355
  383.5 212.7 %reduce-scatter.3.cloned.1.call-done = f32[32,128]{1,0:T(8,128)} async-done(((f32[32,4096]{1,0:T(8,128)}), f32[32,128]{1,0:T(8,128)}) %reduce-scatter.3.cloned.1.call-update) | async-done | bytes 16400 | tf_op jit(solution)/shard_map/reduce_scatter | solution.py:204
  596.2 0.7 fusion.339
  597.5 125.4 %psum.29 = f32[2,2,32,32]{2,3,1,0:T(8,128)S(1)} all-reduce(f32[2,2,32,32]{2,3,1,0:T(8,128)S(1)} %pad_maximum_fusion.2), channel_id=1, replica_groups=mesh['row'=32,'col'=16] {'row','col'}, use_global_device_ids=true, to_apply=%region_2.4 | all-reduce | flops 4096 | bytes 32768 | tf_op jit(solution)/shard_map/psum | solution.py:206
  722.9 403.5 %while.36 = (s32[]{:T(128)}, f32[32,64]{0,1:T(8,128)S(1)}, s32[]{:T(128)}, s32[]{:T(128)}, s32[]{:T(128)}, /*index=5*/s32[]{:T(128)}, s32[]{:T(128)}, f32[]{:T(128)}, f32[]{:T(128)}, f32[]{:T(128)}, /*index=10*/f32[]{:T(128)}) while((s32[]{:T(128)}, f32[32,64]{0,1:T(8,128)S(1)}, s32[]{:T(128)}, s32[]{:T(128)}, ...), condition=%wide.region_6.8_spmd.clone.clone, body=%wide.region_3.7_spmd.clone.clone.sunk | while | flops 87498 | bytes 50118 | solution.py:82
  748.8 0.7 iota_reduce_fusion.4
  1129.8 103.1 %all_gather.7 = f32[32,4096]{1,0:T(8,128)S(1)} all-gather(f32[32,128]{1,0:T(8,128)S(1)} %get-tuple-element.280), channel_id=1, replica_groups=mesh['row'=32,'col'=16] {'row'}, dimensions={1}, use_global_device_ids=true | all-gather | bytes 540672 | tf_op jit(solution)/shard_map/all_gather | solution.py:201
  1234.2 0.8 copy_bitcast_fusion.6
  1235.6 249.9 %all-reduce.5.cloned.1.call-done = f32[32,512]{1,0:T(8,128)} async-done(((f32[32,512]{1,0:T(8,128)}), f32[32,512]{1,0:T(8,128)}) %all-reduce.5.cloned.1.call-update) | async-done | bytes 65552 | tf_op jit(solution)/shard_map/psum | solution.py:202
  1485.5 0.9 fusion.103
  1486.7 1.1 convolution_bitcast_fusion
  1487.7 1.1 add_select_fusion.18
  1488.9 1.1 copy.354
  1491.4 213.1 %reduce-scatter.5.cloned.1.call-done = f32[32,128]{1,0:T(8,128)} async-done(((f32[32,4096]{1,0:T(8,128)}), f32[32,128]{1,0:T(8,128)}) %reduce-scatter.5.cloned.1.call-update) | async-done | bytes 16400 | tf_op jit(solution)/shard_map/reduce_scatter | solution.py:204
  1704.5 0.7 fusion.343
  1705.8 125.7 %psum.31 = f32[2,2,32,32]{2,3,1,0:T(8,128)S(1)} all-reduce(f32[2,2,32,32]{2,3,1,0:T(8,128)S(1)} %pad_maximum_fusion.3), channel_id=1, replica_groups=mesh['row'=32,'col'=16] {'row','col'}, use_global_device_ids=true, to_apply=%region_9.11 | all-reduce | flops 4096 | bytes 32768 | tf_op jit(solution)/shard_map/psum | solution.py:206
  1831.6 403.5 %while.37 = (s32[]{:T(128)}, f32[32,64]{0,1:T(8,128)S(1)}, s32[]{:T(128)}, s32[]{:T(128)}, s32[]{:T(128)}, /*index=5*/s32[]{:T(128)}, s32[]{:T(128)}, f32[]{:T(128)}, f32[]{:T(128)}, f32[]{:T(128)}, /*index=10*/f32[]{:T(128)}) while((s32[]{:T(128)}, f32[32,64]{0,1:T(8,128)S(1)}, s32[]{:T(128)}, s32[]{:T(128)}, ...), condition=%wide.region_13.15_spmd.clone.clone, body=%wide.region_10.14_spmd.clone.clone.sunk | while | flops 87498 | bytes 50118 | solution.py:82
  (714 shorter events, 184.7 us)
Async XLA Ops:
  7.2 116.5 %copy-start = (s32[4,4,128,128]{3,2,1,0:T(8,128)S(1)}, s32[4,4,128,128]{3,2,1,0:T(8,128)}, u32[]{:S(2)}) copy-start(s32[4,4,128,128]{3,2,1,0:T(8,128)} %param.15) | copy-start | bytes 3145732
  7.2 369.3 %all-reduce.3.cloned.1.call-start = ((), (), s32[]{:S(2)}) async-start(), calls=%async_computation.2 | async-start | bytes 131072 | tf_op jit(solution)/shard_map/psum | solution.py:202
  125.7 0.7 copy-start.5
  125.7 0.8 copy-start.6
  125.7 470.4 %reduce-scatter.3.cloned.1.call-start = ((), (), s32[]{:S(2)}) async-start(), calls=%async_computation.3 | async-start | bytes 540672 | tf_op jit(solution)/shard_map/reduce_scatter | solution.py:204
  126.9 0.7 copy-start.7
  128.2 0.7 copy-start.8
  377.4 0.7 copy-start.4
  381.5 1104.0 %all-reduce.5.cloned.1.call-start = ((), (), s32[]{:S(2)}) async-start(), calls=%async_computation.4 | async-start | bytes 131072 | tf_op jit(solution)/shard_map/psum | solution.py:202
  382.0 0.7 copy-start.9
  382.0 0.7 copy-start.10
  382.8 0.7 copy-start.1
  1129.0 0.7 copy-start.2
  1235.0 469.5 %reduce-scatter.5.cloned.1.call-start = ((), (), s32[]{:S(2)}) async-start(), calls=%async_computation.5 | async-start | bytes 540672 | tf_op jit(solution)/shard_map/reduce_scatter | solution.py:204
  2236.6 0.7 copy-start.3
Sparse Core Ops, SparseCore 0:
  125.8 250.6 all-reduce.2
  381.6 214.5 reduce-scatter.2
  1235.1 250.3 all-reduce.4
  1490.1 214.3 reduce-scatter.4
where the time goes:
time: 2250 us; the launch traced here: 2240 us
  waiting for transfers between devices  923 us (41%)
  loops' own time  641 us (28%)
  blocking collectives  469 us (21%)
  other arithmetic  139 us (6%)
  local copies, waits for them, and re-layouts  47.5 us (2%)
    another operation x2, loops' own time, inverse_matrix(): augmented = lax.fori_loop(0, matrix_order, eliminate, augmented)  641 us
    psum x2, waiting for transfers between devices, body(): lax.psum(forward_partial(block_full, tile_values, tile_cols), 'col')  497 us
    reduce_scatter x2, waiting for transfers between devices, body(): lax.psum_scatter(partial_term, 'row', scatter_dimension=1, tiled=True)  426 us
    psum x2, blocking collectives, body(): lax.psum(jnp.stack([digit_pair(gram_local(current_own, applied)), digit_p...  251 us
    all_gather x2, blocking collectives, body(): block_full = lax.all_gather(current, 'row', axis=1, tiled=True)  218 us
    another operation x64, other arithmetic, eliminate(): pivot_row_id = jnp.where(jnp.any(usable), jnp.argmax(usable), column)  46.5 us
  transfers between devices with their start and end apart: 4, of which 4 were waited for; matrix products, arithmetic and copies ran while one was open for 0% of the time, Pallas kernels for 0%

commit v1 on v0

v1 whole, which is shorter than its diff:
```python
import functools

import jax
import jax.numpy as jnp
from jax import lax
from jax.experimental import pallas as pl
from jax.experimental.pallas import tpu as pltpu
from jax.sharding import Mesh
from jax.sharding import PartitionSpec as P

PRIME = 65521
modulus = 65521.0
BLOCK = 32
TILE = 128
ROW_Z, ROW_Y = 8, 4
COL_Z, COL_X, COL_C = 2, 4, 2
ROWS = ROW_Z * ROW_Y
SMALL = 8
PART = ROW_Z * BLOCK

f32, bf16, i32 = jnp.float32, jnp.bfloat16, jnp.int32


def modp(x):
    top = jnp.floor(x * (1.0 / 65536.0))
    rest = x - top * modulus
    return jnp.where(rest >= modulus, rest - modulus, rest)


def digits(x):
    top = jnp.floor(x * (1.0 / 256.0))
    return top, x - top * 256.0


def stack_digits(x):
    top, low = digits(x)
    return jnp.concatenate([top, low], axis=0).astype(bf16)


def fold_two(top, low):
    return modp(modp(modp(top) * 256.0) + low)


def fold_three(upper, middle, lower):
    return modp(modp(upper) * 15.0 + modp(modp(middle) * 256.0) + lower)


def dot(a, b):
    return lax.dot_general(a, b, (((1,), (0,)), ((), ())), preferred_element_type=f32)


def dot_t(a, b):
    return lax.dot_general(a, b, (((1,), (1,)), ((), ())), preferred_element_type=f32)


def product(left, right):
    stacked = stack_digits(left)
    top, low = digits(right)
    by_top = dot(stacked, top.astype(bf16))
    by_low = dot(stacked, low.astype(bf16))
    return fold_three(by_top[:BLOCK], by_top[BLOCK:] + by_low[:BLOCK], by_low[BLOCK:])


def self_product(stacked):
    all_four = dot_t(stacked, stacked)
    by_top = all_four[:, :BLOCK]
    by_low = all_four[:, BLOCK:]
    return fold_three(by_top[:BLOCK], by_top[BLOCK:] + by_low[:BLOCK], by_low[BLOCK:])


def pack(matrix):
    return jnp.concatenate([matrix[8 * k : 8 * k + 8] for k in range(4)], axis=1)


def unpack(packed):
    return jnp.concatenate([packed[:, 32 * k : 32 * k + 32] for k in range(4)], axis=0)


def eye():
    rows = lax.broadcasted_iota(i32, (BLOCK, BLOCK), 0)
    cols = lax.broadcasted_iota(i32, (BLOCK, BLOCK), 1)
    return (rows == cols).astype(f32)


def shrink(x):
    return lax.shift_right_logical(x, 16) * 15 + (x & 65535)


def settle(x):
    return jnp.where(x >= PRIME, x - PRIME, x)


def mulmod(a, b):
    return settle(shrink(shrink(a * b)))


def power(a):
    def fourth_up(x):
        for unused in range(4):
            x = mulmod(x, x)
        return x

    a2 = mulmod(a, a)
    a3 = mulmod(a2, a)
    a6 = mulmod(a3, a3)
    a12 = mulmod(a6, a6)
    a14 = mulmod(a12, a2)
    a15 = mulmod(a12, a3)
    a255 = mulmod(fourth_up(a15), a15)
    high = mulmod(fourth_up(a255), a14)
    return mulmod(fourth_up(high), a15)


def to_int(x):
    return x.astype(i32)


def lane_sum(x):
    return to_int(jnp.sum(x.astype(f32), axis=1, keepdims=True))


def sublane_sum(x):
    return to_int(jnp.sum(x.astype(f32), axis=0, keepdims=True))


def invert(gram, out_ref):
    wide = (BLOCK, 128)
    rows = lax.broadcasted_iota(i32, wide, 0)
    lanes = lax.broadcasted_iota(i32, wide, 1)
    start = jnp.concatenate([gram, eye(), jnp.zeros((BLOCK, 64), f32)], axis=1)
    start = to_int(start)

    matrix = start
    least = jnp.full((1, 1), PRIME, i32)
    for c in range(BLOCK):
        pivot_row = matrix[c : c + 1, :]
        pivot = matrix[c : c + 1, c : c + 1]
        column = matrix[:, c : c + 1]
        least = jnp.minimum(least, pivot)
        kept = shrink(matrix * jnp.broadcast_to(pivot, wide))
        taken = shrink(jnp.broadcast_to(column, wide) * jnp.broadcast_to(pivot_row, wide))
        updated = settle(shrink(kept - taken + 17 * PRIME))
        matrix = jnp.where(rows == c, matrix, updated)
    diagonal = lane_sum(jnp.where(rows == lanes, matrix, 0))
    scale = power(jnp.broadcast_to(diagonal, wide))
    out_ref[...] = mulmod(matrix, scale)[:, BLOCK : 2 * BLOCK].astype(f32)

    @pl.when(jnp.min(least.astype(f32)) == 0.0)
    def _():
        def eliminate(c, m):
            column = lane_sum(jnp.where(lanes == c, m, 0))
            row_ids = lax.broadcasted_iota(i32, (BLOCK, 1), 0)
            usable = (column != 0) & (row_ids >= c)
            at = jnp.min(jnp.where(usable, row_ids, BLOCK).astype(f32), axis=0, keepdims=True)
            at = to_int(at)
            at = jnp.where(at == BLOCK, c, at)
            at = jnp.broadcast_to(at, wide)
            pivot_row = jnp.broadcast_to(sublane_sum(jnp.where(rows == at, m, 0)), wide)
            current = jnp.broadcast_to(sublane_sum(jnp.where(rows == c, m, 0)), wide)
            swapped = jnp.where(rows == c, pivot_row, jnp.where(rows == at, current, m))
            pivot = jnp.broadcast_to(lane_sum(jnp.where(lanes == c, pivot_row, 0)), wide)
            scaled = mulmod(pivot_row, power(pivot))
            factors = jnp.broadcast_to(lane_sum(jnp.where(lanes == c, swapped, 0)), wide)
            reduced = settle(swapped - mulmod(factors, scaled) + PRIME)
            return jnp.where(rows == c, scaled, reduced)

        m = lax.fori_loop(0, BLOCK, eliminate, start)
        out_ref[...] = m[:, BLOCK : 2 * BLOCK].astype(f32)


def call(kernel, outs, args, smem=(), scratch=(), flops=0):
    specs = [
        pl.BlockSpec(memory_space=pltpu.SMEM if n in smem else pltpu.VMEM)
        for n in range(len(args))
    ]
    shapes = [jax.ShapeDtypeStruct(s, t) for s, t in outs]
    got = pl.pallas_call(
        kernel,
        out_shape=shapes,
        in_specs=specs,
        out_specs=[pl.BlockSpec(memory_space=pltpu.VMEM)] * len(shapes),
        scratch_shapes=list(scratch),
        compiler_params=pltpu.CompilerParams(vmem_limit_bytes=32 * 2**20),
        cost_estimate=pl.CostEstimate(flops=flops, bytes_accessed=4 * 2**20, transcendentals=0),
    )(*args)
    return got


def tile_at(t):
    return lax.rem(t, ROW_Y), lax.div(t, ROW_Y) * BLOCK


def forward(cols_ref, block_ref, tiles_ref, out_ref, count, slots):
    for r in range(count):
        total = None
        for s in range(slots):
            part, row = tile_at(cols_ref[r, s])
            picked = block_ref[part, pl.ds(pl.multiple_of(row, BLOCK), BLOCK), :]
            term = dot_t(stack_digits(picked), tiles_ref[r * slots + s])
            total = term if total is None else total + term
        out_ref[r * BLOCK : (r + 1) * BLOCK, :] = fold_two(total[:BLOCK], total[BLOCK:])


def backward(cols_ref, projected, tiles_ref, sums_ref, out_ref, count, slots):
    sums_ref[...] = jnp.zeros_like(sums_ref)
    gram = jnp.zeros((BLOCK, BLOCK), f32)
    for r in range(count):
        stacked = stack_digits(projected[r])
        gram = gram + self_product(stacked)
        for s in range(slots):
            t = cols_ref[r, s]
            sums_ref[t] += dot(stacked, tiles_ref[r * slots + s])
    for t in range(ROWS):
        whole = sums_ref[t]
        y, z = t % ROW_Y, t // ROW_Y
        out_ref[y, z * BLOCK : (z + 1) * BLOCK, :] = fold_two(whole[:BLOCK], whole[BLOCK:])
    packed = pack(modp(gram))
    for y in range(ROW_Y):
        out_ref[y, PART : PART + SMALL, :] = packed


def forward_first_kernel(count, slots, cols_ref, block_ref, tiles_ref, out_ref):
    forward(cols_ref, block_ref, tiles_ref, out_ref, count, slots)


def forward_second_kernel(count, slots, cols_ref, block_ref, tiles_ref, out_ref):
    forward(cols_ref, block_ref, tiles_ref, out_ref, count, slots)
    square = block_ref[0, PART : PART + SMALL, :]
    for y in range(1, ROW_Y):
        square = square + block_ref[y, PART : PART + SMALL, :]
    out_ref[count * BLOCK : count * BLOCK + SMALL, :] = modp(square)


def backward_first_kernel(count, slots, cols_ref, own_ref, other_ref, tiles_ref, out_ref, y_ref, sums_ref):
    projected = []
    for r in range(count):
        at = slice(r * BLOCK, (r + 1) * BLOCK)
        value = modp(own_ref[at, :] + other_ref[at, :])
        y_ref[at, :] = value
        projected.append(value)
    backward(cols_ref, projected, tiles_ref, sums_ref, out_ref, count, slots)


def backward_second_kernel(
    count, slots, cols_ref, own_ref, other_ref, tiles_ref, gram_ref, inv_y_ref, inv_x_ref, old_ref, shifted_ref,
    out_ref, next_ref, result_ref, third_ref, sums_ref,
):
    small = slice(count * BLOCK, count * BLOCK + SMALL)
    square = unpack(modp(own_ref[small, :] + other_ref[small, :]))
    both = modp(square + gram_ref[...])
    projected = []
    for r in range(count):
        at = slice(r * BLOCK, (r + 1) * BLOCK)
        value = modp(own_ref[at, :] + other_ref[at, :])
        projected.append(modp(value - product(both, inv_y_ref[at, :]) + modulus))
    backward(cols_ref, projected, tiles_ref, sums_ref, out_ref, count, slots)
    following = modp(shifted_ref[...] - product(both, inv_x_ref[...]) + modulus)
    next_ref[...] = following
    result_ref[...] = following / modulus
    third_ref[...] = product(both, old_ref[...])


def sum_y_kernel(in_ref, out_ref):
    for z in range(ROW_Z):
        at = slice(z * BLOCK, (z + 1) * BLOCK)
        total = in_ref[0, at, :]
        for y in range(1, ROW_Y):
            total = total + in_ref[y, at, :]
        out_ref[z, :BLOCK, :] = total
    small = slice(PART, PART + SMALL)
    total = in_ref[0, small, :]
    for y in range(1, ROW_Y):
        total = total + in_ref[y, small, :]
    for z in range(ROW_Z):
        out_ref[z, BLOCK:, :] = total


def summed(in_ref):
    total = in_ref[0]
    for k in range(1, in_ref.shape[0]):
        total = total + in_ref[k]
    return modp(total)


def third_kernel(gram_ref, square_ref, inverse_ref, older_ref, now_ref, earliest_ref, out_ref):
    gram = gram_ref[...]
    middle = modp(eye() - product(inverse_ref[...], gram) + modulus)
    third = product(product(modp(square_ref[...] + gram), middle), older_ref[...])
    out_ref[...] = modp(now_ref[...] - product(third, earliest_ref[...]) + modulus)


def shift_kernel(in_ref, inverse_ref, earlier_ref, base_ref, out_ref, shifted_ref, gram_ref):
    total = summed(in_ref)
    applied = total[:BLOCK]
    gram = unpack(total[BLOCK:])
    gram_ref[...] = gram
    second = product(gram, inverse_ref[...])
    shifted = modp(applied + base_ref[...] + (modulus - product(second, earlier_ref[...])))
    shifted_ref[...] = shifted
    square = pack(self_product(stack_digits(applied)))
    for z in range(ROW_Z):
        out_ref[z, :BLOCK, :] = shifted
        out_ref[z, BLOCK:, :] = square


def spread_y_kernel(in_ref, out_ref):
    square = in_ref[0, BLOCK:, :]
    for z in range(1, ROW_Z):
        square = square + in_ref[z, BLOCK:, :]
    square = modp(square)
    for y in range(ROW_Y):
        for z in range(ROW_Z):
            out_ref[y, z * BLOCK : (z + 1) * BLOCK, :] = in_ref[z, :BLOCK, :]
        out_ref[y, PART:, :] = square


def inverse_kernel(
    count, gram_ref, older_ref, y_ref, now_ref, earlier_ref, inv_y_ref, inv_x_ref, old_ref, inverse_ref
):
    gram = gram_ref[...]
    invert(gram, inverse_ref)
    inverse = inverse_ref[...]
    for r in range(count):
        at = slice(r * BLOCK, (r + 1) * BLOCK)
        inv_y_ref[at, :] = product(inverse, y_ref[at, :])
    inv_x_ref[...] = product(inverse, now_ref[...])
    middle = modp(eye() - product(inverse, gram) + modulus)
    old_ref[...] = product(product(middle, older_ref[...]), earlier_ref[...])


def ending_kernel(in_ref, next_ref, inv_x_ref, third_ref, out_ref, base_ref, inv_next_ref, gram_ref, inverse_ref):
    total = summed(in_ref)
    applied = total[:BLOCK]
    gram = unpack(total[BLOCK:])
    gram_ref[...] = gram
    square = pack(self_product(stack_digits(applied)))
    for k in range(out_ref.shape[0]):
        out_ref[k] = square
    following = next_ref[...]
    minus = modp(product(gram, inv_x_ref[...]) + third_ref[...])
    base_ref[...] = modp(applied + following + (modulus - minus))
    invert(gram, inverse_ref)
    inv_next_ref[...] = product(inverse_ref[...], following)


def relay_kernel(in_ref, out_ref):
    total = summed(in_ref)
    for k in range(out_ref.shape[0]):
        out_ref[k] = total


def last_kernel(in_ref, gram_ref, base_ref, inv_next_ref, out_ref):
    both = modp(unpack(summed(in_ref)) + gram_ref[...])
    out_ref[...] = modp(base_ref[...] - product(both, inv_next_ref[...]) + modulus) / modulus


def exchange(parts, axis):
    return lax.all_to_all(parts, axis, 0, 0, tiled=True)


def flip(x, axis):
    return lax.ppermute(x, axis, [(0, 1), (1, 0)])


def sum_core_x(partial):
    pair = partial + flip(partial, "c")
    return jnp.sum(exchange(jnp.broadcast_to(pair[None], (COL_X, *pair.shape)), "x"), axis=0)


def body(entries, tile_cols, block_now, block_prev, block_prev2, gram_prev, square_prev, inverse_prev, inverse_prev2):
    count, slots = tile_cols.shape
    length = count * BLOCK
    tiles = entries.astype(bf16).reshape(count * slots, TILE, TILE)
    current, earlier, earliest = (b.astype(f32) for b in (block_now, block_prev, block_prev2))
    gram_old, square_old, inverse_old, inverse_older = (
        m.astype(f32) for m in (gram_prev, square_prev, inverse_prev, inverse_prev2)
    )
    shard = (BLOCK, TILE)
    small = (BLOCK, BLOCK)
    sums = [pltpu.VMEM((ROWS, 2 * BLOCK, TILE), f32)]

    along_z = exchange(jnp.broadcast_to(current[None], (ROW_Z, *shard)), "zl")
    block = exchange(jnp.broadcast_to(along_z.reshape(1, PART, TILE), (ROW_Y, PART, TILE)), "y")
    [partial] = call(
        functools.partial(forward_first_kernel, count, slots), [((length, TILE), f32)], [tile_cols, block, tiles], smem=(0,)
    )
    own = sum_core_x(partial)
    other = flip(own, "zh")
    [base] = call(
        third_kernel, [(shard, f32)],
        [gram_old, square_old, inverse_old, inverse_older, current, earliest],
        flops=10**9,
    )

    spread, projected = call(
        functools.partial(backward_first_kernel, count, slots),
        [((ROW_Y, PART + SMALL, TILE), f32), ((length, TILE), f32)],
        [tile_cols, own, other, tiles], smem=(0,), scratch=sums,
    )
    chunks = (ROW_Z, BLOCK + SMALL, TILE)
    [by_z] = call(sum_y_kernel, [(chunks, f32)], [exchange(spread, "y")])
    out, shifted, gram_now = call(
        shift_kernel, [(chunks, f32), (shard, f32), (small, f32)],
        [exchange(by_z, "zl"), inverse_old, earlier, base],
    )

    [spread] = call(spread_y_kernel, [((ROW_Y, PART + SMALL, TILE), f32)], [exchange(out, "zl")])
    [partial] = call(
        functools.partial(forward_second_kernel, count, slots),
        [((length + SMALL, TILE), f32)], [tile_cols, exchange(spread, "y"), tiles], smem=(0,),
    )
    own = sum_core_x(partial)
    other = flip(own, "zh")
    inv_y, inv_x, old, inverse_now = call(
        functools.partial(inverse_kernel, count),
        [((length, TILE), f32), (shard, f32), (shard, f32), (small, f32)],
        [gram_now, inverse_old, projected, current, earlier],
        flops=10**9,
    )
    spread, following, result, third = call(
        functools.partial(backward_second_kernel, count, slots),
        [((ROW_Y, PART + SMALL, TILE), f32), (shard, f32), (shard, f32), (shard, f32)],
        [tile_cols, own, other, tiles, gram_now, inv_y, inv_x, old, shifted], smem=(0,), scratch=sums,
    )
    [by_z] = call(sum_y_kernel, [(chunks, f32)], [exchange(spread, "y")])
    near = ROW_Y * COL_X * COL_C
    far = COL_Z * ROW_Z
    out, base, inv_next, gram_next, inverse_next = call(
        ending_kernel,
        [((near, SMALL, TILE), f32), (shard, f32), (shard, f32), (small, f32), (small, f32)],
        [exchange(by_z, "zl"), following, inv_x, third],
    )
    [out] = call(relay_kernel, [((far, SMALL, TILE), f32)], [exchange(out, ("y", "x", "c"))])
    [later] = call(last_kernel, [(shard, f32)], [exchange(out, ("zh", "zl")), gram_next, base, inv_next])
    return result, later


def solution(mesh):
    fine = Mesh(mesh.devices.reshape(ROW_Z, ROW_Y, COL_Z, COL_X, COL_C), ("zl", "y", "zh", "x", "c"))
    row, col = ("zl", "y"), ("zh", "x", "c")
    columns = P(None, (*col, *row))
    return jax.shard_map(
        body,
        mesh=fine,
        in_specs=(P(row, col, None, None), P(row, col), columns, columns, columns, P(), P(), P(), P()),
        out_specs=(columns, columns),
        check_vma=False,
    )
```

time: 2250 us -> 227 us (0.10)
  waiting for transfers between devices: 923 us -> 23 us
  loops' own time: 641 us -> 0 us
  blocking collectives: 469 us -> 134 us
  other arithmetic: 139 us -> 0.9 us
  starting transfers between devices: 0.34 us -> 44.2 us
  local copies, waits for them, and re-layouts: 47.5 us -> 4.44 us
    another operation x2 -> x0, loops' own time: 641 us -> none  [inverse_matrix(): augmented = lax.fori_loop(0, matrix_order, eliminate, augmented)]
    psum x2 -> x0, waiting for transfers between devices: 497 us -> none  [body(): lax.psum(forward_partial(block_full, tile_values, tile_cols), 'col')]
    reduce_scatter x2 -> x0, waiting for transfers between devices: 426 us -> none  [body(): lax.psum_scatter(partial_term, 'row', scatter_dimension=1, tiled=True)]
    psum x2 -> x0, blocking collectives: 251 us -> none  [body(): lax.psum(jnp.stack([digit_pair(gram_local(current_own, applied)), digit_p...]
    all_gather x2 -> x0, blocking collectives: 218 us -> none  [body(): block_full = lax.all_gather(current, 'row', axis=1, tiled=True)]
    all_to_all x0 -> x10, blocking collectives: none -> 134 us  [exchange(): return lax.all_to_all(parts, axis, 0, 0, tiled=True)]
    another operation x79 -> x0, other arithmetic: 48.9 us -> none  [the longest x64 46.5 us: eliminate(): pivot_row_id = jnp.where(jnp.any(usable), jnp.argmax(usable), column)]
    eq x128 -> x0, other arithmetic: 41.6 us -> none  [the longest x64 41.2 us: eliminate(): return jnp.where((row_numbers == column)[:, None], scaled[None, :], reduced)]
  transfers between devices with their start and end apart: 4 -> 6, of which waited for: 4 -> 6; matrix products, arithmetic and copies ran while one was open for 0% -> 0% of each run, Pallas kernels for 0% -> 3%
where the time goes in v1:
time: 227 us; the launch traced here: 226 us
  blocking collectives  134 us (59%)
  starting transfers between devices  44.2 us (19%)
  waiting for transfers between devices  23 us (10%)
  Pallas kernels  18.7 us (8%)
  local copies, waits for them, and re-layouts  4.44 us (2%)
    all_to_all x10, blocking collectives, exchange(): return lax.all_to_all(parts, axis, 0, 0, tiled=True)  134 us
    ppermute x4, starting transfers between devices, flip(): return lax.ppermute(x, axis, [(0, 1), (1, 0)])  34.6 us
    pallas_call x13, Pallas kernels, call(): pl.pallas_call(kernel, out_shape=shapes, in_specs=specs, out_specs=[pl.Bl...  18.7 us
    all_to_all x2, waiting for transfers between devices, exchange(): return lax.all_to_all(parts, axis, 0, 0, tiled=True)  13.2 us
    ppermute x4, waiting for transfers between devices, flip(): return lax.ppermute(x, axis, [(0, 1), (1, 0)])  9.76 us
    all_to_all x2, starting transfers between devices, exchange(): return lax.all_to_all(parts, axis, 0, 0, tiled=True)  9.53 us
  transfers between devices with their start and end apart: 6, of which 6 were waited for; matrix products, arithmetic and copies ran while one was open for 0% of the time, Pallas kernels for 3%

profile of v1, /device:TPU:1, one launch (start us, length us, event | category | flops | bytes accessed | tf_op | source)
XLA Modules:
  0.0 225.9 jit_solution(441485216694744778)
XLA Ops:
  1.4 23.3 %all_to_all.60 = f32[8,32,128]{2,1,0:T(8,128)S(1)} all-to-all(f32[8,32,128]{2,1,0:T(8,128)S(1)} %broadcast_in_dim.10), channel_id=1, replica_groups=mesh['zl'=8,'y'=4,'zh'=2,'x'=4,'c'=2] {'zl'}, dimensions={0} | all-to-all | bytes 262144 | tf_op jit(solution)/shard_map/all_to_all | solution.py:358
  25.5 4.2 %all-to-all-start.1 = ((f32[4,256,128]{2,1,0:T(8,128)}), f32[4,256,128]{2,1,0:T(8,128)S(1)}, u32[]{:S(2)}, u32[]{:S(2)}) async-start(f32[4,256,128]{2,1,0:T(8,128)} %broadcast_in_dim.12), calls=%async_computation.1 | async-start | bytes 1048576 | tf_op jit(solution)/shard_map/all_to_all | solution.py:358
  29.8 6.8 %all-to-all-done.1.block_ref = f32[4,256,128]{2,1,0:T(8,128)S(1)} async-done(((f32[4,256,128]{2,1,0:T(8,128)}), f32[4,256,128]{2,1,0:T(8,128)S(1)}, u32[]{:S(2)}, u32[]{:S(2)}) %all-to-all-start.1) | async-done | bytes 524320 | tf_op jit(solution)/shard_map/all_to_all | solution.py:358
  37.7 5.9 %collective-permute-start = (f32[128,128]{1,0:T(8,128)S(1)}, f32[128,128]{1,0:T(8,128)S(1)}, u32[]{:S(2)}, u32[]{:S(2)}) collective-permute-start(f32[128,128]{1,0:T(8,128)S(1)} %shard_map.104), channel_id=1, source_target_pairs={{0,1},{1,0},{2,3},{3,2},{4,5},{5,4},{6,7},{7,6},{8,9},{9,8},{10,11... | collective-permute-start | bytes 196616 | tf_op jit(solution)/shard_map/ppermute | solution.py:362
  44.5 9.6 %all_to_all.61 = f32[4,128,128]{2,1,0:T(8,128)S(1)} all-to-all(f32[4,128,128]{2,1,0:T(8,128)S(1)} %broadcast_in_dim.13), channel_id=1, replica_groups=mesh['zl'=8,'y'=4,'zh'=2,'x'=4,'c'=2] {'x'}, dimensions={0} | all-to-all | bytes 524288 | tf_op jit(solution)/shard_map/all_to_all | solution.py:358
  54.2 7.9 %collective-permute-start.1 = (f32[128,128]{1,0:T(8,128)S(1)}, f32[128,128]{1,0:T(8,128)S(1)}, u32[]{:S(2)}, u32[]{:S(2)}) collective-permute-start(f32[128,128]{1,0:T(8,128)S(1)} %reduce_sum.18.own_ref), channel_id=1, source_target_pairs={{0,8},{8,0},{1,9},{9,1},{2,10},{10,2},{3,11},{11,3},{4,12},{12,4},... | collective-permute-start | bytes 196616 | tf_op jit(solution)/shard_map/ppermute | solution.py:362
  62.1 5.8 %collective-permute-done.1.other_ref = f32[128,128]{1,0:T(8,128)S(1)} collective-permute-done((f32[128,128]{1,0:T(8,128)S(1)}, f32[128,128]{1,0:T(8,128)S(1)}, u32[]{:S(2)}, u32[]{:S(2)}) %collective-permute-start.1) | collective-permute-done | bytes 65568 | tf_op jit(solution)/shard_map/ppermute | solution.py:362
  67.9 1.4 shard_map.105
  69.3 9.4 %all_to_all.62.in_ref = f32[4,264,128]{2,1,0:T(8,128)S(1)} all-to-all(f32[4,264,128]{2,1,0:T(8,128)S(1)} %get-tuple-element.18), channel_id=1, replica_groups=mesh['zl'=8,'y'=4,'zh'=2,'x'=4,'c'=2] {'y'}, dimensions={0} | all-to-all | bytes 1081344 | tf_op jit(solution)/shard_map/all_to_all | solution.py:358
  79.4 5.4 %all-to-all-start.4 = ((f32[8,40,128]{2,1,0:T(8,128)}), f32[8,40,128]{2,1,0:T(8,128)S(1)}, u32[]{:S(2)}, u32[]{:S(2)}) async-start(f32[8,40,128]{2,1,0:T(8,128)} %shard_map.106), calls=%async_computation.4 | async-start | bytes 327680 | tf_op jit(solution)/shard_map/all_to_all | solution.py:358
  89.0 6.4 %all-to-all-done.4.in_ref = f32[8,40,128]{2,1,0:T(8,128)S(1)} async-done(((f32[8,40,128]{2,1,0:T(8,128)}), f32[8,40,128]{2,1,0:T(8,128)S(1)}, u32[]{:S(2)}, u32[]{:S(2)}) %all-to-all-start.4) | async-done | bytes 163872 | tf_op jit(solution)/shard_map/all_to_all | solution.py:358
  95.8 13.9 %all_to_all.63.in_ref = f32[8,40,128]{2,1,0:T(8,128)S(1)} all-to-all(f32[8,40,128]{2,1,0:T(8,128)S(1)} %get-tuple-element.19), channel_id=1, replica_groups=mesh['zl'=8,'y'=4,'zh'=2,'x'=4,'c'=2] {'zl'}, dimensions={0} | all-to-all | bytes 327680 | tf_op jit(solution)/shard_map/all_to_all | solution.py:358
  109.7 9.6 %all_to_all.64.block_ref = f32[4,264,128]{2,1,0:T(8,128)S(1)} all-to-all(f32[4,264,128]{2,1,0:T(8,128)S(1)} %shard_map.109), channel_id=1, replica_groups=mesh['zl'=8,'y'=4,'zh'=2,'x'=4,'c'=2] {'y'}, dimensions={0} | all-to-all | bytes 1081344 | tf_op jit(solution)/shard_map/all_to_all | solution.py:358
  120.3 12.9 %collective-permute-start.2 = (f32[136,128]{1,0:T(8,128)S(1)}, f32[136,128]{1,0:T(8,128)S(1)}, u32[]{:S(2)}, u32[]{:S(2)}) collective-permute-start(f32[136,128]{1,0:T(8,128)S(1)} %shard_map.110), channel_id=1, source_target_pairs={{0,1},{1,0},{2,3},{3,2},{4,5},{5,4},{6,7},{7,6},{8,9},{9,8},{10,11... | collective-permute-start | bytes 208904 | tf_op jit(solution)/shard_map/ppermute | solution.py:362
  134.2 9.0 %all_to_all.65 = f32[4,136,128]{2,1,0:T(8,128)S(1)} all-to-all(f32[4,136,128]{2,1,0:T(8,128)S(1)} %broadcast_in_dim.14), channel_id=1, replica_groups=mesh['zl'=8,'y'=4,'zh'=2,'x'=4,'c'=2] {'x'}, dimensions={0} | all-to-all | bytes 557056 | tf_op jit(solution)/shard_map/all_to_all | solution.py:358
  143.2 7.8 %collective-permute-start.3 = (f32[136,128]{1,0:T(8,128)S(1)}, f32[136,128]{1,0:T(8,128)S(1)}, u32[]{:S(2)}, u32[]{:S(2)}) collective-permute-start(f32[136,128]{1,0:T(8,128)S(1)} %reduce_sum.19.own_ref), channel_id=1, source_target_pairs={{0,8},{8,0},{1,9},{9,1},{2,10},{10,2},{3,11},{11,3},{4,12},{12,4},... | collective-permute-start | bytes 208904 | tf_op jit(solution)/shard_map/ppermute | solution.py:362
  151.0 5.3 %shard_map.111 = (f32[128,128]{1,0:T(8,128)S(1)}, f32[32,128]{1,0:T(8,128)S(1)}, f32[32,128]{1,0:T(8,128)S(1)}, f32[32,32]{1,0:T(8,128)}) custom-call(f32[32,32]{1,0:T(8,128)S(1)} %get-tuple-element.20.gram_ref, f32[32,32]{1,0:T(8,128)S(1)} %convert_element_type.26.inverse_ref.older_ref, f32[128,128]{1,0:T(8,128)S(1)} %get-tuple-element.21.y_ref, ...), custom_call_target="tpu_custom_call" | custom-call | flops 1000000000 | bytes 4194304 | tf_op jit(solution)/shard_map/pallas_call | solution.py:177
  156.3 2.2 collective-permute-done.3.other_ref
  158.5 2.3 %shard_map.112 = (f32[4,264,128]{2,1,0:T(8,128)S(1)}, f32[32,128]{1,0:T(8,128)S(1)}, f32[32,128]{1,0:T(8,128)}, f32[32,128]{1,0:T(8,128)S(1)}) custom-call(s32[4,4]{1,0:T(4,128)S(1)} %copy-done, f32[136,128]{1,0:T(8,128)S(1)} %reduce_sum.19.own_ref, f32[136,128]{1,0:T(8,128)S(1)} %collective-permute-done.3.other_ref, bf16[16,128,128]{2,1,0:T(8,128)(2,1)S(1)} %bitcast.5, ...), custom_call_target="tpu_custom_call" | custom-call | bytes 4194304 | tf_op jit(solution)/shard_map/pallas_call | solution.py:177
  160.8 9.4 %all_to_all.66.in_ref = f32[4,264,128]{2,1,0:T(8,128)S(1)} all-to-all(f32[4,264,128]{2,1,0:T(8,128)S(1)} %get-tuple-element.27), channel_id=1, replica_groups=mesh['zl'=8,'y'=4,'zh'=2,'x'=4,'c'=2] {'y'}, dimensions={0} | all-to-all | bytes 1081344 | tf_op jit(solution)/shard_map/all_to_all | solution.py:358
  170.2 17.3 %all_to_all.67.in_ref = f32[8,40,128]{2,1,0:T(8,128)S(1)} all-to-all(f32[8,40,128]{2,1,0:T(8,128)S(1)} %shard_map.113), channel_id=1, replica_groups=mesh['zl'=8,'y'=4,'zh'=2,'x'=4,'c'=2] {'zl'}, dimensions={0} | all-to-all | bytes 327680 | tf_op jit(solution)/shard_map/all_to_all | solution.py:358
  187.5 5.0 %shard_map.114 = (f32[32,8,128]{2,1,0:T(8,128)S(1)}, f32[32,128]{1,0:T(8,128)S(1)}, f32[32,128]{1,0:T(8,128)S(1)}, f32[32,32]{1,0:T(8,128)S(1)}, f32[32,32]{1,0:T(8,128)}) custom-call(f32[8,40,128]{2,1,0:T(8,128)S(1)} %all_to_all.67.in_ref, f32[32,128]{1,0:T(8,128)S(1)} %get-tuple-element.28.next_ref, f32[32,128]{1,0:T(8,128)S(1)} %get-tuple-element.23.inv_x_ref, ...), custom_call_target="tpu_custom_call" | custom-call | bytes 4194304 | tf_op jit(solution)/shard_map/pallas_call | solution.py:177
  192.5 13.8 %all_to_all.68.in_ref = f32[32,8,128]{2,1,0:T(8,128)S(1)} all-to-all(f32[32,8,128]{2,1,0:T(8,128)S(1)} %get-tuple-element.30), channel_id=1, replica_groups=mesh['zl'=8,'y'=4,'zh'=2,'x'=4,'c'=2] {'y','x','c'}, dimensions={0} | all-to-all | bytes 262144 | tf_op jit(solution)/shard_map/all_to_all | solution.py:358
  206.3 18.7 %all_to_all.69.in_ref = f32[16,8,128]{2,1,0:T(8,128)S(1)} all-to-all(f32[16,8,128]{2,1,0:T(8,128)S(1)} %shard_map.115), channel_id=1, replica_groups=mesh['zl'=8,'y'=4,'zh'=2,'x'=4,'c'=2] {'zh','zl'}, dimensions={0} | all-to-all | bytes 131072 | tf_op jit(solution)/shard_map/all_to_all | solution.py:358
  (43 shorter events, 11.8 us)
Async XLA Ops:
  1.4 28.4 %copy-start.1 = (s32[4,4,128,128]{3,2,1,0:T(8,128)S(1)}, s32[4,4,128,128]{3,2,1,0:T(8,128)}, u32[]{:S(2)}) copy-start(s32[4,4,128,128]{3,2,1,0:T(8,128)} %param.9) | copy-start | bytes 3145732
  25.5 11.1 %all-to-all-start.1 = ((f32[4,256,128]{2,1,0:T(8,128)}), f32[4,256,128]{2,1,0:T(8,128)S(1)}, u32[]{:S(2)}, u32[]{:S(2)}) async-start(f32[4,256,128]{2,1,0:T(8,128)} %broadcast_in_dim.12), calls=%async_computation.1 | async-start | bytes 1048576 | tf_op jit(solution)/shard_map/all_to_all | solution.py:358
  29.7 6.9 %copy-start = (s32[4,4]{1,0:T(4,128)S(1)}, s32[4,4]{1,0:T(4,128)}, u32[]{:S(2)}) copy-start(s32[4,4]{1,0:T(4,128)} %cols_ref.7) | copy-start | bytes 196
  37.7 6.8 %collective-permute-start = (f32[128,128]{1,0:T(8,128)S(1)}, f32[128,128]{1,0:T(8,128)S(1)}, u32[]{:S(2)}, u32[]{:S(2)}) collective-permute-start(f32[128,128]{1,0:T(8,128)S(1)} %shard_map.104), channel_id=1, source_target_pairs={{0,1},{1,0},{2,3},{3,2},{4,5},{5,4},{6,7},{7,6},{8,9},{9,8},{10,11... | collective-permute-start | bytes 196616 | tf_op jit(solution)/shard_map/ppermute | solution.py:362
  54.2 13.7 %collective-permute-start.1 = (f32[128,128]{1,0:T(8,128)S(1)}, f32[128,128]{1,0:T(8,128)S(1)}, u32[]{:S(2)}, u32[]{:S(2)}) collective-permute-start(f32[128,128]{1,0:T(8,128)S(1)} %reduce_sum.18.own_ref), channel_id=1, source_target_pairs={{0,8},{8,0},{1,9},{9,1},{2,10},{10,2},{3,11},{11,3},{4,12},{12,4},... | collective-permute-start | bytes 196616 | tf_op jit(solution)/shard_map/ppermute | solution.py:362
  79.4 5.4 %copy-start.2 = (s32[32,32]{1,0:T(8,128)S(1)}, s32[32,32]{1,0:T(8,128)}, u32[]{:S(2)}) copy-start(s32[32,32]{1,0:T(8,128)} %param.16) | copy-start | bytes 12292
  79.4 16.0 %all-to-all-start.4 = ((f32[8,40,128]{2,1,0:T(8,128)}), f32[8,40,128]{2,1,0:T(8,128)S(1)}, u32[]{:S(2)}, u32[]{:S(2)}) async-start(f32[8,40,128]{2,1,0:T(8,128)} %shard_map.106), calls=%async_computation.4 | async-start | bytes 327680 | tf_op jit(solution)/shard_map/all_to_all | solution.py:358
  84.7 0.7 copy-start.3
  85.5 0.7 copy-start.4
  86.2 0.7 copy-start.5
  86.9 0.7 copy-start.6
  87.6 0.7 copy-start.7
  120.3 13.8 %collective-permute-start.2 = (f32[136,128]{1,0:T(8,128)S(1)}, f32[136,128]{1,0:T(8,128)S(1)}, u32[]{:S(2)}, u32[]{:S(2)}) collective-permute-start(f32[136,128]{1,0:T(8,128)S(1)} %shard_map.110), channel_id=1, source_target_pairs={{0,1},{1,0},{2,3},{3,2},{4,5},{5,4},{6,7},{7,6},{8,9},{9,8},{10,11... | collective-permute-start | bytes 208904 | tf_op jit(solution)/shard_map/ppermute | solution.py:362
  143.2 15.4 %collective-permute-start.3 = (f32[136,128]{1,0:T(8,128)S(1)}, f32[136,128]{1,0:T(8,128)S(1)}, u32[]{:S(2)}, u32[]{:S(2)}) collective-permute-start(f32[136,128]{1,0:T(8,128)S(1)} %reduce_sum.19.own_ref), channel_id=1, source_target_pairs={{0,8},{8,0},{1,9},{9,1},{2,10},{10,2},{3,11},{11,3},{4,12},{12,4},... | collective-permute-start | bytes 208904 | tf_op jit(solution)/shard_map/ppermute | solution.py:362

commit v2 on v1

--- a/solution.py
+++ b/solution.py
@@ -83,11 +83,12 @@
 
 
 def shrink(x):
-    return lax.shift_right_logical(x, 16) * 15 + (x & 65535)
+    return x - lax.shift_right_logical(x, 16) * PRIME
 
 
 def settle(x):
-    return jnp.where(x >= PRIME, x - PRIME, x)
+    less = x - PRIME
+    return jnp.where(less < 0, x, less)
 
 
 def mulmod(a, b):
@@ -130,17 +131,27 @@
     start = jnp.concatenate([gram, eye(), jnp.zeros((BLOCK, 64), f32)], axis=1)
     start = to_int(start)
 
+    def spread(row, column):
+        return jnp.broadcast_to(matrix[row : row + 1, column : column + 1], wide)
+
+    def small(x):
+        return settle(shrink(x))
+
+    shift = 17 * PRIME
     matrix = start
     least = jnp.full((1, 1), PRIME, i32)
-    for c in range(BLOCK):
-        pivot_row = matrix[c : c + 1, :]
-        pivot = matrix[c : c + 1, c : c + 1]
-        column = matrix[:, c : c + 1]
-        least = jnp.minimum(least, pivot)
-        kept = shrink(matrix * jnp.broadcast_to(pivot, wide))
-        taken = shrink(jnp.broadcast_to(column, wide) * jnp.broadcast_to(pivot_row, wide))
-        updated = settle(shrink(kept - taken + 17 * PRIME))
-        matrix = jnp.where(rows == c, matrix, updated)
+    for c in range(0, BLOCK, 2):
+        row_a = jnp.broadcast_to(matrix[c : c + 1, :], wide)
+        row_b = jnp.broadcast_to(matrix[c + 1 : c + 2, :], wide)
+        aa, ab, ba, bb = spread(c, c), spread(c, c + 1), spread(c + 1, c), spread(c + 1, c + 1)
+        of_a = jnp.broadcast_to(matrix[:, c : c + 1], wide)
+        of_b = jnp.broadcast_to(matrix[:, c + 1 : c + 2], wide)
+        det = small(shrink(aa * bb) - shrink(ab * ba) + shift)
+        least = jnp.minimum(least, jnp.minimum(aa[:1, :1], det[:1, :1]))
+        new_a = small(shrink(bb * row_a) - shrink(ab * row_b) + shift)
+        new_b = small(shrink(aa * row_b) - shrink(ba * row_a) + shift)
+        updated = small(shrink(matrix * det) - shrink(of_a * new_a) - shrink(of_b * new_b) + 2 * shift)
+        matrix = jnp.where(rows == c, new_a, jnp.where(rows == c + 1, new_b, updated))
     diagonal = lane_sum(jnp.where(rows == lanes, matrix, 0))
     scale = power(jnp.broadcast_to(diagonal, wide))
     out_ref[...] = mulmod(matrix, scale)[:, BLOCK : 2 * BLOCK].astype(f32)
@@ -219,7 +230,9 @@
         out_ref[y, PART : PART + SMALL, :] = packed
 
 
-def forward_first_kernel(count, slots, cols_ref, block_ref, tiles_ref, out_ref):
+def forward_first_kernel(count, slots, cols_ref, block_ref, entries_ref, out_ref, tiles_ref):
+    for n in range(count * slots):
+        tiles_ref[n] = entries_ref[n].astype(f32).astype(bf16)
     forward(cols_ref, block_ref, tiles_ref, out_ref, count, slots)
 
 
@@ -282,11 +295,16 @@
     return modp(total)
 
 
-def third_kernel(gram_ref, square_ref, inverse_ref, older_ref, now_ref, earliest_ref, out_ref):
-    gram = gram_ref[...]
-    middle = modp(eye() - product(inverse_ref[...], gram) + modulus)
-    third = product(product(modp(square_ref[...] + gram), middle), older_ref[...])
-    out_ref[...] = modp(now_ref[...] - product(third, earliest_ref[...]) + modulus)
+def third_kernel(
+    gram_ref, square_ref, inverse_ref, older_ref, now_ref, earlier_ref, earliest_ref, out_ref, float_inverse_ref, float_earlier_ref
+):
+    gram, inverse = gram_ref[...].astype(f32), inverse_ref[...].astype(f32)
+    float_inverse_ref[...] = inverse
+    float_earlier_ref[...] = earlier_ref[...].astype(f32)
+    middle = modp(eye() - product(inverse, gram) + modulus)
+    both = modp(square_ref[...].astype(f32) + gram)
+    third = product(product(both, middle), older_ref[...].astype(f32))
+    out_ref[...] = modp(now_ref[...] - product(third, earliest_ref[...].astype(f32)) + modulus)
 
 
 def shift_kernel(in_ref, inverse_ref, earlier_ref, base_ref, out_ref, shifted_ref, gram_ref):
@@ -362,6 +380,10 @@
     return lax.ppermute(x, axis, [(0, 1), (1, 0)])
 
 
+def together(*arrays):
+    return lax.optimization_barrier(arrays)
+
+
 def sum_core_x(partial):
     pair = partial + flip(partial, "c")
     return jnp.sum(exchange(jnp.broadcast_to(pair[None], (COL_X, *pair.shape)), "x"), axis=0)
@@ -370,27 +392,27 @@
 def body(entries, tile_cols, block_now, block_prev, block_prev2, gram_prev, square_prev, inverse_prev, inverse_prev2):
     count, slots = tile_cols.shape
     length = count * BLOCK
-    tiles = entries.astype(bf16).reshape(count * slots, TILE, TILE)
-    current, earlier, earliest = (b.astype(f32) for b in (block_now, block_prev, block_prev2))
-    gram_old, square_old, inverse_old, inverse_older = (
-        m.astype(f32) for m in (gram_prev, square_prev, inverse_prev, inverse_prev2)
-    )
+    stored = entries.reshape(count * slots, TILE, TILE)
+    current = block_now.astype(f32)
     shard = (BLOCK, TILE)
     small = (BLOCK, BLOCK)
     sums = [pltpu.VMEM((ROWS, 2 * BLOCK, TILE), f32)]
 
     along_z = exchange(jnp.broadcast_to(current[None], (ROW_Z, *shard)), "zl")
     block = exchange(jnp.broadcast_to(along_z.reshape(1, PART, TILE), (ROW_Y, PART, TILE)), "y")
-    [partial] = call(
-        functools.partial(forward_first_kernel, count, slots), [((length, TILE), f32)], [tile_cols, block, tiles], smem=(0,)
+    partial, tiles = call(
+        functools.partial(forward_first_kernel, count, slots),
+        [((length, TILE), f32), (stored.shape, bf16)], [tile_cols, block, stored], smem=(0,),
     )
     own = sum_core_x(partial)
     other = flip(own, "zh")
-    [base] = call(
-        third_kernel, [(shard, f32)],
-        [gram_old, square_old, inverse_old, inverse_older, current, earliest],
-        flops=10**9,
-    )
+    own, *given = together(
+        own, gram_prev, square_prev, inverse_prev, inverse_prev2, current, block_prev, block_prev2
+    )
+    base, inverse_old, earlier = call(
+        third_kernel, [(shard, f32), (small, f32), (shard, f32)], given, flops=10**9
+    )
+    other, base, inverse_old, earlier = together(other, base, inverse_old, earlier)
 
     spread, projected = call(
         functools.partial(backward_first_kernel, count, slots),
@@ -427,11 +449,11 @@
     far = COL_Z * ROW_Z
     out, base, inv_next, gram_next, inverse_next = call(
         ending_kernel,
-        [((near, SMALL, TILE), f32), (shard, f32), (shard, f32), (small, f32), (small, f32)],
+        [((far, SMALL, TILE), f32), (shard, f32), (shard, f32), (small, f32), (small, f32)],
         [exchange(by_z, "zl"), following, inv_x, third],
     )
-    [out] = call(relay_kernel, [((far, SMALL, TILE), f32)], [exchange(out, ("y", "x", "c"))])
-    [later] = call(last_kernel, [(shard, f32)], [exchange(out, ("zh", "zl")), gram_next, base, inv_next])
+    [out] = call(relay_kernel, [((near, SMALL, TILE), f32)], [exchange(out, ("zh", "zl"))])
+    [later] = call(last_kernel, [(shard, f32)], [exchange(out, ("y", "x", "c")), gram_next, base, inv_next])
     return result, later
 
 

time: 227 us -> 225 us (level)
  blocking collectives: 134 us -> 164 us
  waiting for transfers between devices: 23 us -> 9.23 us
  starting transfers between devices: 44.2 us -> 34.8 us
  local copies, waits for them, and re-layouts: 4.44 us -> 0.12 us
  Pallas kernels: 18.7 us -> 14.8 us
    all_to_all x10 -> x12, blocking collectives: 134 us -> 164 us  [exchange(): return lax.all_to_all(parts, axis, 0, 0, tiled=True)]
    all_to_all x2 -> x0, waiting for transfers between devices: 13.2 us -> none  [exchange(): return lax.all_to_all(parts, axis, 0, 0, tiled=True)]
    all_to_all x2 -> x0, starting transfers between devices: 9.53 us -> none  [exchange(): return lax.all_to_all(parts, axis, 0, 0, tiled=True)]
    pallas_call x13, Pallas kernels: 18.7 us -> 14.8 us  [call(): pl.pallas_call(kernel, out_shape=shapes, in_specs=specs, out_specs=[pl.Bl...]
    unnamed x16, local copies, waits for them, and re-layouts: 3.56 us -> 0.04 us
  transfers between devices with their start and end apart: 6 -> 4, of which waited for: 6 -> 4; matrix products, arithmetic and copies ran while one was open for 0% -> 0% of each run, Pallas kernels for 3% -> 2%
where the time goes in v2:
time: 225 us; the launch traced here: 224 us
  blocking collectives  164 us (73%)
  starting transfers between devices  34.8 us (15%)
  Pallas kernels  14.8 us (7%)
  waiting for transfers between devices  9.23 us (4%)
    all_to_all x12, blocking collectives, exchange(): return lax.all_to_all(parts, axis, 0, 0, tiled=True)  164 us
    ppermute x4, starting transfers between devices, flip(): return lax.ppermute(x, axis, [(0, 1), (1, 0)])  34.8 us
    pallas_call x13, Pallas kernels, call(): pl.pallas_call(kernel, out_shape=shapes, in_specs=specs, out_specs=[pl.Bl...  14.8 us
    ppermute x4, waiting for transfers between devices, flip(): return lax.ppermute(x, axis, [(0, 1), (1, 0)])  9.23 us
  transfers between devices with their start and end apart: 4, of which 4 were waited for; matrix products, arithmetic and copies ran while one was open for 0% of the time, Pallas kernels for 2%

profile of v2, /device:TPU:1, one launch (start us, length us, event | category | flops | bytes accessed | tf_op | source)
XLA Modules:
  0.0 224.1 jit_solution(17703109016064251042)
XLA Ops:
  1.4 23.3 %all_to_all.60 = f32[8,32,128]{2,1,0:T(8,128)S(1)} all-to-all(f32[8,32,128]{2,1,0:T(8,128)S(1)} %broadcast_in_dim.10), channel_id=1, replica_groups=mesh['zl'=8,'y'=4,'zh'=2,'x'=4,'c'=2] {'zl'}, dimensions={0} | all-to-all | bytes 262144 | tf_op jit(solution)/shard_map/all_to_all | solution.py:376
  24.8 10.9 %all_to_all.61.block_ref = f32[4,256,128]{2,1,0:T(8,128)S(1)} all-to-all(f32[4,256,128]{2,1,0:T(8,128)S(1)} %broadcast_in_dim.12), channel_id=1, replica_groups=mesh['zl'=8,'y'=4,'zh'=2,'x'=4,'c'=2] {'y'}, dimensions={0} | all-to-all | bytes 1048576 | tf_op jit(solution)/shard_map/all_to_all | solution.py:376
  35.7 1.1 shard_map.104
  36.7 5.9 %collective-permute-start = (f32[128,128]{1,0:T(8,128)S(1)}, f32[128,128]{1,0:T(8,128)S(1)}, u32[]{:S(2)}, u32[]{:S(2)}) collective-permute-start(f32[128,128]{1,0:T(8,128)S(1)} %get-tuple-element.35), channel_id=1, source_target_pairs={{0,1},{1,0},{2,3},{3,2},{4,5},{5,4},{6,7},{7,6},{8,9},{9,8},{10,11... | collective-permute-start | bytes 196616 | tf_op jit(solution)/shard_map/ppermute | solution.py:380
  43.6 9.6 %all_to_all.62 = f32[4,128,128]{2,1,0:T(8,128)S(1)} all-to-all(f32[4,128,128]{2,1,0:T(8,128)S(1)} %broadcast_in_dim.13), channel_id=1, replica_groups=mesh['zl'=8,'y'=4,'zh'=2,'x'=4,'c'=2] {'x'}, dimensions={0} | all-to-all | bytes 524288 | tf_op jit(solution)/shard_map/all_to_all | solution.py:376
  53.3 8.1 %collective-permute-start.1 = (f32[128,128]{1,0:T(8,128)S(1)}, f32[128,128]{1,0:T(8,128)S(1)}, u32[]{:S(2)}, u32[]{:S(2)}) collective-permute-start(f32[128,128]{1,0:T(8,128)S(1)} %reduce_sum.18.own_ref), channel_id=1, source_target_pairs={{0,8},{8,0},{1,9},{9,1},{2,10},{10,2},{3,11},{11,3},{4,12},{12,4},... | collective-permute-start | bytes 196616 | tf_op jit(solution)/shard_map/ppermute | solution.py:380
  62.1 5.1 %collective-permute-done.1.other_ref = f32[128,128]{1,0:T(8,128)S(1)} collective-permute-done((f32[128,128]{1,0:T(8,128)S(1)}, f32[128,128]{1,0:T(8,128)S(1)}, u32[]{:S(2)}, u32[]{:S(2)}) %collective-permute-start.1) | collective-permute-done | bytes 65568 | tf_op jit(solution)/shard_map/ppermute | solution.py:380
  67.1 1.4 shard_map.106
  68.5 9.4 %all_to_all.63.in_ref = f32[4,264,128]{2,1,0:T(8,128)S(1)} all-to-all(f32[4,264,128]{2,1,0:T(8,128)S(1)} %get-tuple-element.49), channel_id=1, replica_groups=mesh['zl'=8,'y'=4,'zh'=2,'x'=4,'c'=2] {'y'}, dimensions={0} | all-to-all | bytes 1081344 | tf_op jit(solution)/shard_map/all_to_all | solution.py:376
  77.9 15.7 %all_to_all.64.in_ref = f32[8,40,128]{2,1,0:T(8,128)S(1)} all-to-all(f32[8,40,128]{2,1,0:T(8,128)S(1)} %shard_map.107), channel_id=1, replica_groups=mesh['zl'=8,'y'=4,'zh'=2,'x'=4,'c'=2] {'zl'}, dimensions={0} | all-to-all | bytes 327680 | tf_op jit(solution)/shard_map/all_to_all | solution.py:376
  94.0 13.9 %all_to_all.65.in_ref = f32[8,40,128]{2,1,0:T(8,128)S(1)} all-to-all(f32[8,40,128]{2,1,0:T(8,128)S(1)} %get-tuple-element.53), channel_id=1, replica_groups=mesh['zl'=8,'y'=4,'zh'=2,'x'=4,'c'=2] {'zl'}, dimensions={0} | all-to-all | bytes 327680 | tf_op jit(solution)/shard_map/all_to_all | solution.py:376
  107.9 9.6 %all_to_all.66.block_ref = f32[4,264,128]{2,1,0:T(8,128)S(1)} all-to-all(f32[4,264,128]{2,1,0:T(8,128)S(1)} %shard_map.109), channel_id=1, replica_groups=mesh['zl'=8,'y'=4,'zh'=2,'x'=4,'c'=2] {'y'}, dimensions={0} | all-to-all | bytes 1081344 | tf_op jit(solution)/shard_map/all_to_all | solution.py:376
  117.5 1.0 shard_map.110
  118.5 12.9 %collective-permute-start.2 = (f32[136,128]{1,0:T(8,128)S(1)}, f32[136,128]{1,0:T(8,128)S(1)}, u32[]{:S(2)}, u32[]{:S(2)}) collective-permute-start(f32[136,128]{1,0:T(8,128)S(1)} %shard_map.110), channel_id=1, source_target_pairs={{0,1},{1,0},{2,3},{3,2},{4,5},{5,4},{6,7},{7,6},{8,9},{9,8},{10,11... | collective-permute-start | bytes 208904 | tf_op jit(solution)/shard_map/ppermute | solution.py:380
  132.4 9.0 %all_to_all.67 = f32[4,136,128]{2,1,0:T(8,128)S(1)} all-to-all(f32[4,136,128]{2,1,0:T(8,128)S(1)} %broadcast_in_dim.14), channel_id=1, replica_groups=mesh['zl'=8,'y'=4,'zh'=2,'x'=4,'c'=2] {'x'}, dimensions={0} | all-to-all | bytes 557056 | tf_op jit(solution)/shard_map/all_to_all | solution.py:376
  141.4 7.9 %collective-permute-start.3 = (f32[136,128]{1,0:T(8,128)S(1)}, f32[136,128]{1,0:T(8,128)S(1)}, u32[]{:S(2)}, u32[]{:S(2)}) collective-permute-start(f32[136,128]{1,0:T(8,128)S(1)} %reduce_sum.19.own_ref), channel_id=1, source_target_pairs={{0,8},{8,0},{1,9},{9,1},{2,10},{10,2},{3,11},{11,3},{4,12},{12,4},... | collective-permute-start | bytes 208904 | tf_op jit(solution)/shard_map/ppermute | solution.py:380
  149.3 3.6 %shard_map.111 = (f32[128,128]{1,0:T(8,128)S(1)}, f32[32,128]{1,0:T(8,128)S(1)}, f32[32,128]{1,0:T(8,128)S(1)}, f32[32,32]{1,0:T(8,128)}) custom-call(f32[32,32]{1,0:T(8,128)S(1)} %get-tuple-element.54.gram_ref, f32[32,32]{1,0:T(8,128)S(1)} %get-tuple-element.50.inverse_ref.older_ref, f32[128,128]{1,0:T(8,128)S(1)} %get-tuple-element.55.y_ref, ...), custom_call_target="tpu_custom_call" | custom-call | flops 1000000000 | bytes 4194304 | tf_op jit(solution)/shard_map/pallas_call | solution.py:188
  152.9 2.4 %collective-permute-done.3.other_ref = f32[136,128]{1,0:T(8,128)S(1)} collective-permute-done((f32[136,128]{1,0:T(8,128)S(1)}, f32[136,128]{1,0:T(8,128)S(1)}, u32[]{:S(2)}, u32[]{:S(2)}) %collective-permute-start.3) | collective-permute-done | bytes 69664 | tf_op jit(solution)/shard_map/ppermute | solution.py:380
  155.3 2.3 %shard_map.112 = (f32[4,264,128]{2,1,0:T(8,128)S(1)}, f32[32,128]{1,0:T(8,128)S(1)}, f32[32,128]{1,0:T(8,128)}, f32[32,128]{1,0:T(8,128)S(1)}) custom-call(s32[4,4]{1,0:T(4,128)S(1)} %copy-done.1, f32[136,128]{1,0:T(8,128)S(1)} %reduce_sum.19.own_ref, f32[136,128]{1,0:T(8,128)S(1)} %collective-permute-done.3.other_ref, ...), custom_call_target="tpu_custom_call" | custom-call | bytes 4194304 | tf_op jit(solution)/shard_map/pallas_call | solution.py:188
  157.6 10.4 %all_to_all.68.in_ref = f32[4,264,128]{2,1,0:T(8,128)S(1)} all-to-all(f32[4,264,128]{2,1,0:T(8,128)S(1)} %get-tuple-element.61), channel_id=1, replica_groups=mesh['zl'=8,'y'=4,'zh'=2,'x'=4,'c'=2] {'y'}, dimensions={0} | all-to-all | bytes 1081344 | tf_op jit(solution)/shard_map/all_to_all | solution.py:376
  168.0 17.7 %all_to_all.69.in_ref = f32[8,40,128]{2,1,0:T(8,128)S(1)} all-to-all(f32[8,40,128]{2,1,0:T(8,128)S(1)} %shard_map.113), channel_id=1, replica_groups=mesh['zl'=8,'y'=4,'zh'=2,'x'=4,'c'=2] {'zl'}, dimensions={0} | all-to-all | bytes 327680 | tf_op jit(solution)/shard_map/all_to_all | solution.py:376
  185.7 3.4 %shard_map.114 = (f32[16,8,128]{2,1,0:T(8,128)S(1)}, f32[32,128]{1,0:T(8,128)S(1)}, f32[32,128]{1,0:T(8,128)S(1)}, f32[32,32]{1,0:T(8,128)S(1)}, f32[32,32]{1,0:T(8,128)}) custom-call(f32[8,40,128]{2,1,0:T(8,128)S(1)} %all_to_all.69.in_ref, f32[32,128]{1,0:T(8,128)S(1)} %get-tuple-element.62.next_ref, f32[32,128]{1,0:T(8,128)S(1)} %get-tuple-element.57.inv_x_ref, ...), custom_call_target="tpu_custom_call" | custom-call | bytes 4194304 | tf_op jit(solution)/shard_map/pallas_call | solution.py:188
  189.1 18.7 %all_to_all.70.in_ref = f32[16,8,128]{2,1,0:T(8,128)S(1)} all-to-all(f32[16,8,128]{2,1,0:T(8,128)S(1)} %get-tuple-element.64), channel_id=1, replica_groups=mesh['zl'=8,'y'=4,'zh'=2,'x'=4,'c'=2] {'zh','zl'}, dimensions={0} | all-to-all | bytes 131072 | tf_op jit(solution)/shard_map/all_to_all | solution.py:376
  207.8 15.4 %all_to_all.71.in_ref = f32[32,8,128]{2,1,0:T(8,128)S(1)} all-to-all(f32[32,8,128]{2,1,0:T(8,128)S(1)} %shard_map.115), channel_id=1, replica_groups=mesh['zl'=8,'y'=4,'zh'=2,'x'=4,'c'=2] {'y','x','c'}, dimensions={0} | all-to-all | bytes 262144 | tf_op jit(solution)/shard_map/all_to_all | solution.py:376
  (34 shorter events, 4.7 us)
Async XLA Ops:
  1.4 34.3 %copy-start = (s32[4,4,128,128]{3,2,1,0:T(8,128)S(1)}, s32[4,4,128,128]{3,2,1,0:T(8,128)}, u32[]{:S(2)}) copy-start(s32[4,4,128,128]{3,2,1,0:T(8,128)} %param.9) | copy-start | bytes 3145732
  24.7 10.9 %copy-start.1 = (s32[4,4]{1,0:T(4,128)S(1)}, s32[4,4]{1,0:T(4,128)}, u32[]{:S(2)}) copy-start(s32[4,4]{1,0:T(4,128)} %cols_ref.7) | copy-start | bytes 196
  36.7 6.8 %collective-permute-start = (f32[128,128]{1,0:T(8,128)S(1)}, f32[128,128]{1,0:T(8,128)S(1)}, u32[]{:S(2)}, u32[]{:S(2)}) collective-permute-start(f32[128,128]{1,0:T(8,128)S(1)} %get-tuple-element.35), channel_id=1, source_target_pairs={{0,1},{1,0},{2,3},{3,2},{4,5},{5,4},{6,7},{7,6},{8,9},{9,8},{10,11... | collective-permute-start | bytes 196616 | tf_op jit(solution)/shard_map/ppermute | solution.py:380
  53.2 8.1 %copy-start.2 = (s32[32,32]{1,0:T(8,128)S(1)}, s32[32,32]{1,0:T(8,128)}, u32[]{:S(2)}) copy-start(s32[32,32]{1,0:T(8,128)} %gram_ref) | copy-start | bytes 12292
  53.2 8.1 %copy-start.3 = (s32[32,32]{1,0:T(8,128)S(1)}, s32[32,32]{1,0:T(8,128)}, u32[]{:S(2)}) copy-start(s32[32,32]{1,0:T(8,128)} %square_ref) | copy-start | bytes 12292
  53.2 8.2 %copy-start.4 = (s32[32,32]{1,0:T(8,128)S(1)}, s32[32,32]{1,0:T(8,128)}, u32[]{:S(2)}) copy-start(s32[32,32]{1,0:T(8,128)} %inverse_ref) | copy-start | bytes 12292
  53.2 8.2 %copy-start.5 = (s32[32,32]{1,0:T(8,128)S(1)}, s32[32,32]{1,0:T(8,128)}, u32[]{:S(2)}) copy-start(s32[32,32]{1,0:T(8,128)} %older_ref) | copy-start | bytes 12292
  53.2 8.2 %copy-start.6 = (s32[32,128]{1,0:T(8,128)S(1)}, s32[32,128]{1,0:T(8,128)}, u32[]{:S(2)}) copy-start(s32[32,128]{1,0:T(8,128)} %earlier_ref) | copy-start | bytes 49156
  53.2 8.2 %copy-start.7 = (s32[32,128]{1,0:T(8,128)S(1)}, s32[32,128]{1,0:T(8,128)}, u32[]{:S(2)}) copy-start(s32[32,128]{1,0:T(8,128)} %earliest_ref) | copy-start | bytes 49156
  53.3 13.9 %collective-permute-start.1 = (f32[128,128]{1,0:T(8,128)S(1)}, f32[128,128]{1,0:T(8,128)S(1)}, u32[]{:S(2)}, u32[]{:S(2)}) collective-permute-start(f32[128,128]{1,0:T(8,128)S(1)} %reduce_sum.18.own_ref), channel_id=1, source_target_pairs={{0,8},{8,0},{1,9},{9,1},{2,10},{10,2},{3,11},{11,3},{4,12},{12,4},... | collective-permute-start | bytes 196616 | tf_op jit(solution)/shard_map/ppermute | solution.py:380
  118.5 13.8 %collective-permute-start.2 = (f32[136,128]{1,0:T(8,128)S(1)}, f32[136,128]{1,0:T(8,128)S(1)}, u32[]{:S(2)}, u32[]{:S(2)}) collective-permute-start(f32[136,128]{1,0:T(8,128)S(1)} %shard_map.110), channel_id=1, source_target_pairs={{0,1},{1,0},{2,3},{3,2},{4,5},{5,4},{6,7},{7,6},{8,9},{9,8},{10,11... | collective-permute-start | bytes 208904 | tf_op jit(solution)/shard_map/ppermute | solution.py:380
  141.4 13.9 %collective-permute-start.3 = (f32[136,128]{1,0:T(8,128)S(1)}, f32[136,128]{1,0:T(8,128)S(1)}, u32[]{:S(2)}, u32[]{:S(2)}) collective-permute-start(f32[136,128]{1,0:T(8,128)S(1)} %reduce_sum.19.own_ref), channel_id=1, source_target_pairs={{0,8},{8,0},{1,9},{9,1},{2,10},{10,2},{3,11},{11,3},{4,12},{12,4},... | collective-permute-start | bytes 208904 | tf_op jit(solution)/shard_map/ppermute | solution.py:380

commit v3 on v2

--- a/solution.py
+++ b/solution.py
@@ -255,22 +255,18 @@
 
 
 def backward_second_kernel(
-    count, slots, cols_ref, own_ref, other_ref, tiles_ref, gram_ref, inv_y_ref, inv_x_ref, old_ref, shifted_ref,
-    out_ref, next_ref, result_ref, third_ref, sums_ref,
+    count, slots, cols_ref, own_ref, other_ref, tiles_ref, gram_ref, inv_y_ref, out_ref, both_ref, sums_ref
 ):
     small = slice(count * BLOCK, count * BLOCK + SMALL)
     square = unpack(modp(own_ref[small, :] + other_ref[small, :]))
     both = modp(square + gram_ref[...])
+    both_ref[...] = both
     projected = []
     for r in range(count):
         at = slice(r * BLOCK, (r + 1) * BLOCK)
         value = modp(own_ref[at, :] + other_ref[at, :])
         projected.append(modp(value - product(both, inv_y_ref[at, :]) + modulus))
     backward(cols_ref, projected, tiles_ref, sums_ref, out_ref, count, slots)
-    following = modp(shifted_ref[...] - product(both, inv_x_ref[...]) + modulus)
-    next_ref[...] = following
-    result_ref[...] = following / modulus
-    third_ref[...] = product(both, old_ref[...])
 
 
 def sum_y_kernel(in_ref, out_ref):
@@ -346,7 +342,9 @@
     old_ref[...] = product(product(middle, older_ref[...]), earlier_ref[...])
 
 
-def ending_kernel(in_ref, next_ref, inv_x_ref, third_ref, out_ref, base_ref, inv_next_ref, gram_ref, inverse_ref):
+def ending_kernel(
+    in_ref, both_ref, shifted_ref, inv_x_ref, old_ref, out_ref, result_ref, base_ref, gram_ref, inverse_ref, inv_next_ref
+):
     total = summed(in_ref)
     applied = total[:BLOCK]
     gram = unpack(total[BLOCK:])
@@ -354,8 +352,10 @@
     square = pack(self_product(stack_digits(applied)))
     for k in range(out_ref.shape[0]):
         out_ref[k] = square
-    following = next_ref[...]
-    minus = modp(product(gram, inv_x_ref[...]) + third_ref[...])
+    both = both_ref[...]
+    following = modp(shifted_ref[...] - product(both, inv_x_ref[...]) + modulus)
+    result_ref[...] = following / modulus
+    minus = modp(product(gram, inv_x_ref[...]) + product(both, old_ref[...]))
     base_ref[...] = modp(applied + following + (modulus - minus))
     invert(gram, inverse_ref)
     inv_next_ref[...] = product(inverse_ref[...], following)
@@ -439,21 +439,21 @@
         [gram_now, inverse_old, projected, current, earlier],
         flops=10**9,
     )
-    spread, following, result, third = call(
+    spread, both = call(
         functools.partial(backward_second_kernel, count, slots),
-        [((ROW_Y, PART + SMALL, TILE), f32), (shard, f32), (shard, f32), (shard, f32)],
-        [tile_cols, own, other, tiles, gram_now, inv_y, inv_x, old, shifted], smem=(0,), scratch=sums,
+        [((ROW_Y, PART + SMALL, TILE), f32), (small, f32)],
+        [tile_cols, own, other, tiles, gram_now, inv_y], smem=(0,), scratch=sums,
     )
     [by_z] = call(sum_y_kernel, [(chunks, f32)], [exchange(spread, "y")])
     near = ROW_Y * COL_X * COL_C
     far = COL_Z * ROW_Z
-    out, base, inv_next, gram_next, inverse_next = call(
+    out, result, base, gram_next, inverse_next, inv_next = call(
         ending_kernel,
-        [((far, SMALL, TILE), f32), (shard, f32), (shard, f32), (small, f32), (small, f32)],
-        [exchange(by_z, "zl"), following, inv_x, third],
-    )
-    [out] = call(relay_kernel, [((near, SMALL, TILE), f32)], [exchange(out, ("zh", "zl"))])
-    [later] = call(last_kernel, [(shard, f32)], [exchange(out, ("y", "x", "c")), gram_next, base, inv_next])
+        [((near, SMALL, TILE), f32), (shard, f32), (shard, f32), (small, f32), (small, f32), (shard, f32)],
+        [exchange(by_z, "zl"), both, shifted, inv_x, old],
+    )
+    [out] = call(relay_kernel, [((far, SMALL, TILE), f32)], [exchange(out, ("y", "x", "c"))])
+    [later] = call(last_kernel, [(shard, f32)], [exchange(out, ("zh", "zl")), gram_next, base, inv_next])
     return result, later
 
 

time: 225 us -> 223 us (level)
  no operation moved by 1% of the time
where the time goes in v3:
time: 223 us; the launch traced here: 222 us
  blocking collectives  162 us (73%)
  starting transfers between devices  34.8 us (16%)
  Pallas kernels  14.2 us (6%)
  waiting for transfers between devices  9.23 us (4%)
    all_to_all x12, blocking collectives, exchange(): return lax.all_to_all(parts, axis, 0, 0, tiled=True)  162 us
    ppermute x4, starting transfers between devices, flip(): return lax.ppermute(x, axis, [(0, 1), (1, 0)])  34.8 us
    pallas_call x13, Pallas kernels, call(): pl.pallas_call(kernel, out_shape=shapes, in_specs=specs, out_specs=[pl.Bl...  14.2 us
    ppermute x4, waiting for transfers between devices, flip(): return lax.ppermute(x, axis, [(0, 1), (1, 0)])  9.23 us
  transfers between devices with their start and end apart: 4, of which 4 were waited for; matrix products, arithmetic and copies ran while one was open for 0% of the time, Pallas kernels for 2%

profile of v3, /device:TPU:1, one launch (start us, length us, event | category | flops | bytes accessed | tf_op | source)
XLA Modules:
  0.0 221.9 jit_solution(1357323711290862268)
XLA Ops:
  1.4 23.3 %all_to_all.60 = f32[8,32,128]{2,1,0:T(8,128)S(1)} all-to-all(f32[8,32,128]{2,1,0:T(8,128)S(1)} %broadcast_in_dim.10), channel_id=1, replica_groups=mesh['zl'=8,'y'=4,'zh'=2,'x'=4,'c'=2] {'zl'}, dimensions={0} | all-to-all | bytes 262144 | tf_op jit(solution)/shard_map/all_to_all | solution.py:376
  24.8 10.9 %all_to_all.61.block_ref = f32[4,256,128]{2,1,0:T(8,128)S(1)} all-to-all(f32[4,256,128]{2,1,0:T(8,128)S(1)} %broadcast_in_dim.12), channel_id=1, replica_groups=mesh['zl'=8,'y'=4,'zh'=2,'x'=4,'c'=2] {'y'}, dimensions={0} | all-to-all | bytes 1048576 | tf_op jit(solution)/shard_map/all_to_all | solution.py:376
  35.7 1.1 shard_map.104
  36.7 5.9 %collective-permute-start = (f32[128,128]{1,0:T(8,128)S(1)}, f32[128,128]{1,0:T(8,128)S(1)}, u32[]{:S(2)}, u32[]{:S(2)}) collective-permute-start(f32[128,128]{1,0:T(8,128)S(1)} %get-tuple-element.34), channel_id=1, source_target_pairs={{0,1},{1,0},{2,3},{3,2},{4,5},{5,4},{6,7},{7,6},{8,9},{9,8},{10,11... | collective-permute-start | bytes 196616 | tf_op jit(solution)/shard_map/ppermute | solution.py:380
  43.6 9.6 %all_to_all.62 = f32[4,128,128]{2,1,0:T(8,128)S(1)} all-to-all(f32[4,128,128]{2,1,0:T(8,128)S(1)} %broadcast_in_dim.13), channel_id=1, replica_groups=mesh['zl'=8,'y'=4,'zh'=2,'x'=4,'c'=2] {'x'}, dimensions={0} | all-to-all | bytes 524288 | tf_op jit(solution)/shard_map/all_to_all | solution.py:376
  53.3 8.1 %collective-permute-start.1 = (f32[128,128]{1,0:T(8,128)S(1)}, f32[128,128]{1,0:T(8,128)S(1)}, u32[]{:S(2)}, u32[]{:S(2)}) collective-permute-start(f32[128,128]{1,0:T(8,128)S(1)} %reduce_sum.18.own_ref), channel_id=1, source_target_pairs={{0,8},{8,0},{1,9},{9,1},{2,10},{10,2},{3,11},{11,3},{4,12},{12,4},... | collective-permute-start | bytes 196616 | tf_op jit(solution)/shard_map/ppermute | solution.py:380
  62.1 5.1 %collective-permute-done.1.other_ref = f32[128,128]{1,0:T(8,128)S(1)} collective-permute-done((f32[128,128]{1,0:T(8,128)S(1)}, f32[128,128]{1,0:T(8,128)S(1)}, u32[]{:S(2)}, u32[]{:S(2)}) %collective-permute-start.1) | collective-permute-done | bytes 65568 | tf_op jit(solution)/shard_map/ppermute | solution.py:380
  67.1 1.4 shard_map.106
  68.5 9.4 %all_to_all.63.in_ref = f32[4,264,128]{2,1,0:T(8,128)S(1)} all-to-all(f32[4,264,128]{2,1,0:T(8,128)S(1)} %get-tuple-element.48), channel_id=1, replica_groups=mesh['zl'=8,'y'=4,'zh'=2,'x'=4,'c'=2] {'y'}, dimensions={0} | all-to-all | bytes 1081344 | tf_op jit(solution)/shard_map/all_to_all | solution.py:376
  77.9 15.7 %all_to_all.64.in_ref = f32[8,40,128]{2,1,0:T(8,128)S(1)} all-to-all(f32[8,40,128]{2,1,0:T(8,128)S(1)} %shard_map.107), channel_id=1, replica_groups=mesh['zl'=8,'y'=4,'zh'=2,'x'=4,'c'=2] {'zl'}, dimensions={0} | all-to-all | bytes 327680 | tf_op jit(solution)/shard_map/all_to_all | solution.py:376
  94.0 13.9 %all_to_all.65.in_ref = f32[8,40,128]{2,1,0:T(8,128)S(1)} all-to-all(f32[8,40,128]{2,1,0:T(8,128)S(1)} %get-tuple-element.52), channel_id=1, replica_groups=mesh['zl'=8,'y'=4,'zh'=2,'x'=4,'c'=2] {'zl'}, dimensions={0} | all-to-all | bytes 327680 | tf_op jit(solution)/shard_map/all_to_all | solution.py:376
  107.9 9.6 %all_to_all.66.block_ref = f32[4,264,128]{2,1,0:T(8,128)S(1)} all-to-all(f32[4,264,128]{2,1,0:T(8,128)S(1)} %shard_map.109), channel_id=1, replica_groups=mesh['zl'=8,'y'=4,'zh'=2,'x'=4,'c'=2] {'y'}, dimensions={0} | all-to-all | bytes 1081344 | tf_op jit(solution)/shard_map/all_to_all | solution.py:376
  117.5 1.0 shard_map.110
  118.5 12.9 %collective-permute-start.2 = (f32[136,128]{1,0:T(8,128)S(1)}, f32[136,128]{1,0:T(8,128)S(1)}, u32[]{:S(2)}, u32[]{:S(2)}) collective-permute-start(f32[136,128]{1,0:T(8,128)S(1)} %shard_map.110), channel_id=1, source_target_pairs={{0,1},{1,0},{2,3},{3,2},{4,5},{5,4},{6,7},{7,6},{8,9},{9,8},{10,11... | collective-permute-start | bytes 208904 | tf_op jit(solution)/shard_map/ppermute | solution.py:380
  132.4 9.0 %all_to_all.67 = f32[4,136,128]{2,1,0:T(8,128)S(1)} all-to-all(f32[4,136,128]{2,1,0:T(8,128)S(1)} %broadcast_in_dim.14), channel_id=1, replica_groups=mesh['zl'=8,'y'=4,'zh'=2,'x'=4,'c'=2] {'x'}, dimensions={0} | all-to-all | bytes 557056 | tf_op jit(solution)/shard_map/all_to_all | solution.py:376
  141.4 7.9 %collective-permute-start.3 = (f32[136,128]{1,0:T(8,128)S(1)}, f32[136,128]{1,0:T(8,128)S(1)}, u32[]{:S(2)}, u32[]{:S(2)}) collective-permute-start(f32[136,128]{1,0:T(8,128)S(1)} %reduce_sum.19.own_ref), channel_id=1, source_target_pairs={{0,8},{8,0},{1,9},{9,1},{2,10},{10,2},{3,11},{11,3},{4,12},{12,4},... | collective-permute-start | bytes 208904 | tf_op jit(solution)/shard_map/ppermute | solution.py:380
  149.3 3.6 %shard_map.111 = (f32[128,128]{1,0:T(8,128)S(1)}, f32[32,128]{1,0:T(8,128)S(1)}, f32[32,128]{1,0:T(8,128)S(1)}, f32[32,32]{1,0:T(8,128)}) custom-call(f32[32,32]{1,0:T(8,128)S(1)} %get-tuple-element.53.gram_ref, f32[32,32]{1,0:T(8,128)S(1)} %get-tuple-element.49.inverse_ref.older_ref, f32[128,128]{1,0:T(8,128)S(1)} %get-tuple-element.54.y_ref, ...), custom_call_target="tpu_custom_call" | custom-call | flops 1000000000 | bytes 4194304 | tf_op jit(solution)/shard_map/pallas_call | solution.py:188
  152.9 2.4 %collective-permute-done.3.other_ref = f32[136,128]{1,0:T(8,128)S(1)} collective-permute-done((f32[136,128]{1,0:T(8,128)S(1)}, f32[136,128]{1,0:T(8,128)S(1)}, u32[]{:S(2)}, u32[]{:S(2)}) %collective-permute-start.3) | collective-permute-done | bytes 69664 | tf_op jit(solution)/shard_map/ppermute | solution.py:380
  155.3 1.7 shard_map.112
  157.0 10.4 %all_to_all.68.in_ref = f32[4,264,128]{2,1,0:T(8,128)S(1)} all-to-all(f32[4,264,128]{2,1,0:T(8,128)S(1)} %get-tuple-element.56), channel_id=1, replica_groups=mesh['zl'=8,'y'=4,'zh'=2,'x'=4,'c'=2] {'y'}, dimensions={0} | all-to-all | bytes 1081344 | tf_op jit(solution)/shard_map/all_to_all | solution.py:376
  167.4 17.7 %all_to_all.69.in_ref = f32[8,40,128]{2,1,0:T(8,128)S(1)} all-to-all(f32[8,40,128]{2,1,0:T(8,128)S(1)} %shard_map.113), channel_id=1, replica_groups=mesh['zl'=8,'y'=4,'zh'=2,'x'=4,'c'=2] {'zl'}, dimensions={0} | all-to-all | bytes 327680 | tf_op jit(solution)/shard_map/all_to_all | solution.py:376
  185.1 3.4 %shard_map.114 = (f32[32,8,128]{2,1,0:T(8,128)S(1)}, f32[32,128]{1,0:T(8,128)}, f32[32,128]{1,0:T(8,128)S(1)}, f32[32,32]{1,0:T(8,128)S(1)}, f32[32,32]{1,0:T(8,128)}, /*index=5*/f32[32,128]{1,0:T(8,128)S(1)}) custom-call(f32[8,40,128]{2,1,0:T(8,128)S(1)} %all_to_all.69.in_ref, f32[32,32]{1,0:T(8,128)S(1)} %get-tuple-element.57.both_ref, ...), custom_call_target="tpu_custom_call" | custom-call | bytes 4194304 | tf_op jit(solution)/shard_map/pallas_call | solution.py:188
  188.5 13.8 %all_to_all.70.in_ref = f32[32,8,128]{2,1,0:T(8,128)S(1)} all-to-all(f32[32,8,128]{2,1,0:T(8,128)S(1)} %get-tuple-element.62), channel_id=1, replica_groups=mesh['zl'=8,'y'=4,'zh'=2,'x'=4,'c'=2] {'y','x','c'}, dimensions={0} | all-to-all | bytes 262144 | tf_op jit(solution)/shard_map/all_to_all | solution.py:376
  202.4 18.7 %all_to_all.71.in_ref = f32[16,8,128]{2,1,0:T(8,128)S(1)} all-to-all(f32[16,8,128]{2,1,0:T(8,128)S(1)} %shard_map.115), channel_id=1, replica_groups=mesh['zl'=8,'y'=4,'zh'=2,'x'=4,'c'=2] {'zh','zl'}, dimensions={0} | all-to-all | bytes 131072 | tf_op jit(solution)/shard_map/all_to_all | solution.py:376
  (34 shorter events, 4.7 us)
Async XLA Ops:
  1.4 34.3 %copy-start = (s32[4,4,128,128]{3,2,1,0:T(8,128)S(1)}, s32[4,4,128,128]{3,2,1,0:T(8,128)}, u32[]{:S(2)}) copy-start(s32[4,4,128,128]{3,2,1,0:T(8,128)} %param.9) | copy-start | bytes 3145732
  24.7 10.9 %copy-start.1 = (s32[4,4]{1,0:T(4,128)S(1)}, s32[4,4]{1,0:T(4,128)}, u32[]{:S(2)}) copy-start(s32[4,4]{1,0:T(4,128)} %cols_ref.7) | copy-start | bytes 196
  36.7 6.8 %collective-permute-start = (f32[128,128]{1,0:T(8,128)S(1)}, f32[128,128]{1,0:T(8,128)S(1)}, u32[]{:S(2)}, u32[]{:S(2)}) collective-permute-start(f32[128,128]{1,0:T(8,128)S(1)} %get-tuple-element.34), channel_id=1, source_target_pairs={{0,1},{1,0},{2,3},{3,2},{4,5},{5,4},{6,7},{7,6},{8,9},{9,8},{10,11... | collective-permute-start | bytes 196616 | tf_op jit(solution)/shard_map/ppermute | solution.py:380
  53.2 8.1 %copy-start.2 = (s32[32,32]{1,0:T(8,128)S(1)}, s32[32,32]{1,0:T(8,128)}, u32[]{:S(2)}) copy-start(s32[32,32]{1,0:T(8,128)} %gram_ref) | copy-start | bytes 12292
  53.2 8.1 %copy-start.3 = (s32[32,32]{1,0:T(8,128)S(1)}, s32[32,32]{1,0:T(8,128)}, u32[]{:S(2)}) copy-start(s32[32,32]{1,0:T(8,128)} %square_ref) | copy-start | bytes 12292
  53.2 8.2 %copy-start.4 = (s32[32,32]{1,0:T(8,128)S(1)}, s32[32,32]{1,0:T(8,128)}, u32[]{:S(2)}) copy-start(s32[32,32]{1,0:T(8,128)} %inverse_ref) | copy-start | bytes 12292
  53.2 8.2 %copy-start.5 = (s32[32,32]{1,0:T(8,128)S(1)}, s32[32,32]{1,0:T(8,128)}, u32[]{:S(2)}) copy-start(s32[32,32]{1,0:T(8,128)} %older_ref) | copy-start | bytes 12292
  53.2 8.2 %copy-start.6 = (s32[32,128]{1,0:T(8,128)S(1)}, s32[32,128]{1,0:T(8,128)}, u32[]{:S(2)}) copy-start(s32[32,128]{1,0:T(8,128)} %earlier_ref) | copy-start | bytes 49156
  53.2 8.2 %copy-start.7 = (s32[32,128]{1,0:T(8,128)S(1)}, s32[32,128]{1,0:T(8,128)}, u32[]{:S(2)}) copy-start(s32[32,128]{1,0:T(8,128)} %earliest_ref) | copy-start | bytes 49156
  53.3 13.9 %collective-permute-start.1 = (f32[128,128]{1,0:T(8,128)S(1)}, f32[128,128]{1,0:T(8,128)S(1)}, u32[]{:S(2)}, u32[]{:S(2)}) collective-permute-start(f32[128,128]{1,0:T(8,128)S(1)} %reduce_sum.18.own_ref), channel_id=1, source_target_pairs={{0,8},{8,0},{1,9},{9,1},{2,10},{10,2},{3,11},{11,3},{4,12},{12,4},... | collective-permute-start | bytes 196616 | tf_op jit(solution)/shard_map/ppermute | solution.py:380
  118.5 13.8 %collective-permute-start.2 = (f32[136,128]{1,0:T(8,128)S(1)}, f32[136,128]{1,0:T(8,128)S(1)}, u32[]{:S(2)}, u32[]{:S(2)}) collective-permute-start(f32[136,128]{1,0:T(8,128)S(1)} %shard_map.110), channel_id=1, source_target_pairs={{0,1},{1,0},{2,3},{3,2},{4,5},{5,4},{6,7},{7,6},{8,9},{9,8},{10,11... | collective-permute-start | bytes 208904 | tf_op jit(solution)/shard_map/ppermute | solution.py:380
  141.4 13.9 %collective-permute-start.3 = (f32[136,128]{1,0:T(8,128)S(1)}, f32[136,128]{1,0:T(8,128)S(1)}, u32[]{:S(2)}, u32[]{:S(2)}) collective-permute-start(f32[136,128]{1,0:T(8,128)S(1)} %reduce_sum.19.own_ref), channel_id=1, source_target_pairs={{0,8},{8,0},{1,9},{9,1},{2,10},{10,2},{3,11},{11,3},{4,12},{12,4},... | collective-permute-start | bytes 208904 | tf_op jit(solution)/shard_map/ppermute | solution.py:380

commit v4 on v3

--- a/solution.py
+++ b/solution.py
@@ -15,6 +15,7 @@
 ROW_Z, ROW_Y = 8, 4
 COL_Z, COL_X, COL_C = 2, 4, 2
 ROWS = ROW_Z * ROW_Y
+AHEAD = 3
 SMALL = 8
 PART = ROW_Z * BLOCK
 
@@ -131,27 +132,33 @@
     start = jnp.concatenate([gram, eye(), jnp.zeros((BLOCK, 64), f32)], axis=1)
     start = to_int(start)
 
-    def spread(row, column):
-        return jnp.broadcast_to(matrix[row : row + 1, column : column + 1], wide)
-
-    def small(x):
-        return settle(shrink(x))
-
-    shift = 17 * PRIME
+    def four(x):
+        return jnp.concatenate([x] * 4, axis=0)
+
+    def row_of(x, c):
+        return jnp.broadcast_to(x[c : c + 1], (8, 128))
+
+    def column_of(x, c):
+        return jnp.broadcast_to(x[:, c : c + 1], wide)
+
     matrix = start
     least = jnp.full((1, 1), PRIME, i32)
-    for c in range(0, BLOCK, 2):
-        row_a = jnp.broadcast_to(matrix[c : c + 1, :], wide)
-        row_b = jnp.broadcast_to(matrix[c + 1 : c + 2, :], wide)
-        aa, ab, ba, bb = spread(c, c), spread(c, c + 1), spread(c + 1, c), spread(c + 1, c + 1)
-        of_a = jnp.broadcast_to(matrix[:, c : c + 1], wide)
-        of_b = jnp.broadcast_to(matrix[:, c + 1 : c + 2], wide)
-        det = small(shrink(aa * bb) - shrink(ab * ba) + shift)
-        least = jnp.minimum(least, jnp.minimum(aa[:1, :1], det[:1, :1]))
-        new_a = small(shrink(bb * row_a) - shrink(ab * row_b) + shift)
-        new_b = small(shrink(aa * row_b) - shrink(ba * row_a) + shift)
-        updated = small(shrink(matrix * det) - shrink(of_a * new_a) - shrink(of_b * new_b) + 2 * shift)
-        matrix = jnp.where(rows == c, new_a, jnp.where(rows == c + 1, new_b, updated))
+    fetched = [column_of(matrix, c) for c in range(AHEAD)]
+    for c in range(BLOCK):
+        factors = fetched[0]
+        pivot = row_of(factors, c)
+        least = jnp.minimum(least, pivot[:1, :1])
+
+        def step(x):
+            kept = shrink(x * four(pivot))
+            taken = shrink(factors * four(row_of(x, c)))
+            return jnp.where(rows == c, x, settle(shrink(kept - taken + 17 * PRIME)))
+
+        waiting = fetched[1:]
+        if c + AHEAD < BLOCK:
+            waiting.append(column_of(matrix, c + AHEAD))
+        fetched = [step(x) for x in waiting]
+        matrix = step(matrix)
     diagonal = lane_sum(jnp.where(rows == lanes, matrix, 0))
     scale = power(jnp.broadcast_to(diagonal, wide))
     out_ref[...] = mulmod(matrix, scale)[:, BLOCK : 2 * BLOCK].astype(f32)
@@ -204,10 +211,14 @@
 def forward(cols_ref, block_ref, tiles_ref, out_ref, count, slots):
     for r in range(count):
         total = None
-        for s in range(slots):
-            part, row = tile_at(cols_ref[r, s])
-            picked = block_ref[part, pl.ds(pl.multiple_of(row, BLOCK), BLOCK), :]
-            term = dot_t(stack_digits(picked), tiles_ref[r * slots + s])
+        for s in range(0, slots, 2):
+            pair = []
+            for k in (s, s + 1):
+                part, row = tile_at(cols_ref[r, k])
+                pair.append(stack_digits(block_ref[part, pl.ds(pl.multiple_of(row, BLOCK), BLOCK), :]))
+            at = r * slots + s
+            stored = jnp.concatenate([tiles_ref[at], tiles_ref[at + 1]], axis=1)
+            term = dot_t(jnp.concatenate(pair, axis=1), stored)
             total = term if total is None else total + term
         out_ref[r * BLOCK : (r + 1) * BLOCK, :] = fold_two(total[:BLOCK], total[BLOCK:])
 
@@ -218,9 +229,11 @@
     for r in range(count):
         stacked = stack_digits(projected[r])
         gram = gram + self_product(stacked)
-        for s in range(slots):
-            t = cols_ref[r, s]
-            sums_ref[t] += dot(stacked, tiles_ref[r * slots + s])
+        for s in range(0, slots, 2):
+            at = r * slots + s
+            terms = dot(stacked, jnp.concatenate([tiles_ref[at], tiles_ref[at + 1]], axis=1))
+            sums_ref[cols_ref[r, s]] += terms[:, :TILE]
+            sums_ref[cols_ref[r, s + 1]] += terms[:, TILE:]
     for t in range(ROWS):
         whole = sums_ref[t]
         y, z = t % ROW_Y, t // ROW_Y

time: 223 us -> 222 us (level)
  waiting for transfers between devices: 9.23 us -> 11.5 us
    ppermute x4, waiting for transfers between devices: 9.23 us -> 11.5 us  [flip(): return lax.ppermute(x, axis, [(0, 1), (1, 0)])]
where the time goes in v4:
time: 222 us; the launch traced here: 221 us
  blocking collectives  160 us (72%)
  starting transfers between devices  34.8 us (16%)
  Pallas kernels  12.4 us (6%)
  waiting for transfers between devices  11.5 us (5%)
    all_to_all x12, blocking collectives, exchange(): return lax.all_to_all(parts, axis, 0, 0, tiled=True)  160 us
    ppermute x4, starting transfers between devices, flip(): return lax.ppermute(x, axis, [(0, 1), (1, 0)])  34.8 us
    pallas_call x13, Pallas kernels, call(): pl.pallas_call(kernel, out_shape=shapes, in_specs=specs, out_specs=[pl.Bl...  12.4 us
    ppermute x4, waiting for transfers between devices, flip(): return lax.ppermute(x, axis, [(0, 1), (1, 0)])  11.5 us
  transfers between devices with their start and end apart: 4, of which 4 were waited for; matrix products, arithmetic and copies ran while one was open for 0% of the time, Pallas kernels for 2%

profile of v4, /device:TPU:1, one launch (start us, length us, event | category | flops | bytes accessed | tf_op | source)
XLA Modules:
  0.0 220.9 jit_solution(4357582864693015671)
XLA Ops:
  1.4 23.3 %all_to_all.60 = f32[8,32,128]{2,1,0:T(8,128)S(1)} all-to-all(f32[8,32,128]{2,1,0:T(8,128)S(1)} %broadcast_in_dim.10), channel_id=1, replica_groups=mesh['zl'=8,'y'=4,'zh'=2,'x'=4,'c'=2] {'zl'}, dimensions={0} | all-to-all | bytes 262144 | tf_op jit(solution)/shard_map/all_to_all | solution.py:389
  24.8 10.9 %all_to_all.61.block_ref = f32[4,256,128]{2,1,0:T(8,128)S(1)} all-to-all(f32[4,256,128]{2,1,0:T(8,128)S(1)} %broadcast_in_dim.12), channel_id=1, replica_groups=mesh['zl'=8,'y'=4,'zh'=2,'x'=4,'c'=2] {'y'}, dimensions={0} | all-to-all | bytes 1048576 | tf_op jit(solution)/shard_map/all_to_all | solution.py:389
  35.7 0.9 shard_map.104
  36.6 5.9 %collective-permute-start = (f32[128,128]{1,0:T(8,128)S(1)}, f32[128,128]{1,0:T(8,128)S(1)}, u32[]{:S(2)}, u32[]{:S(2)}) collective-permute-start(f32[128,128]{1,0:T(8,128)S(1)} %get-tuple-element.34), channel_id=1, source_target_pairs={{0,1},{1,0},{2,3},{3,2},{4,5},{5,4},{6,7},{7,6},{8,9},{9,8},{10,11... | collective-permute-start | bytes 196616 | tf_op jit(solution)/shard_map/ppermute | solution.py:393
  43.4 9.6 %all_to_all.62 = f32[4,128,128]{2,1,0:T(8,128)S(1)} all-to-all(f32[4,128,128]{2,1,0:T(8,128)S(1)} %broadcast_in_dim.13), channel_id=1, replica_groups=mesh['zl'=8,'y'=4,'zh'=2,'x'=4,'c'=2] {'x'}, dimensions={0} | all-to-all | bytes 524288 | tf_op jit(solution)/shard_map/all_to_all | solution.py:389
  53.1 8.1 %collective-permute-start.1 = (f32[128,128]{1,0:T(8,128)S(1)}, f32[128,128]{1,0:T(8,128)S(1)}, u32[]{:S(2)}, u32[]{:S(2)}) collective-permute-start(f32[128,128]{1,0:T(8,128)S(1)} %reduce_sum.18.own_ref), channel_id=1, source_target_pairs={{0,8},{8,0},{1,9},{9,1},{2,10},{10,2},{3,11},{11,3},{4,12},{12,4},... | collective-permute-start | bytes 196616 | tf_op jit(solution)/shard_map/ppermute | solution.py:393
  61.9 5.1 %collective-permute-done.1.other_ref = f32[128,128]{1,0:T(8,128)S(1)} collective-permute-done((f32[128,128]{1,0:T(8,128)S(1)}, f32[128,128]{1,0:T(8,128)S(1)}, u32[]{:S(2)}, u32[]{:S(2)}) %collective-permute-start.1) | collective-permute-done | bytes 65568 | tf_op jit(solution)/shard_map/ppermute | solution.py:393
  67.0 1.4 shard_map.106
  68.4 9.4 %all_to_all.63.in_ref = f32[4,264,128]{2,1,0:T(8,128)S(1)} all-to-all(f32[4,264,128]{2,1,0:T(8,128)S(1)} %get-tuple-element.48), channel_id=1, replica_groups=mesh['zl'=8,'y'=4,'zh'=2,'x'=4,'c'=2] {'y'}, dimensions={0} | all-to-all | bytes 1081344 | tf_op jit(solution)/shard_map/all_to_all | solution.py:389
  77.8 15.7 %all_to_all.64.in_ref = f32[8,40,128]{2,1,0:T(8,128)S(1)} all-to-all(f32[8,40,128]{2,1,0:T(8,128)S(1)} %shard_map.107), channel_id=1, replica_groups=mesh['zl'=8,'y'=4,'zh'=2,'x'=4,'c'=2] {'zl'}, dimensions={0} | all-to-all | bytes 327680 | tf_op jit(solution)/shard_map/all_to_all | solution.py:389
  93.9 13.9 %all_to_all.65.in_ref = f32[8,40,128]{2,1,0:T(8,128)S(1)} all-to-all(f32[8,40,128]{2,1,0:T(8,128)S(1)} %get-tuple-element.52), channel_id=1, replica_groups=mesh['zl'=8,'y'=4,'zh'=2,'x'=4,'c'=2] {'zl'}, dimensions={0} | all-to-all | bytes 327680 | tf_op jit(solution)/shard_map/all_to_all | solution.py:389
  107.8 9.6 %all_to_all.66.block_ref = f32[4,264,128]{2,1,0:T(8,128)S(1)} all-to-all(f32[4,264,128]{2,1,0:T(8,128)S(1)} %shard_map.109), channel_id=1, replica_groups=mesh['zl'=8,'y'=4,'zh'=2,'x'=4,'c'=2] {'y'}, dimensions={0} | all-to-all | bytes 1081344 | tf_op jit(solution)/shard_map/all_to_all | solution.py:389
  118.2 12.9 %collective-permute-start.2 = (f32[136,128]{1,0:T(8,128)S(1)}, f32[136,128]{1,0:T(8,128)S(1)}, u32[]{:S(2)}, u32[]{:S(2)}) collective-permute-start(f32[136,128]{1,0:T(8,128)S(1)} %shard_map.110), channel_id=1, source_target_pairs={{0,1},{1,0},{2,3},{3,2},{4,5},{5,4},{6,7},{7,6},{8,9},{9,8},{10,11... | collective-permute-start | bytes 208904 | tf_op jit(solution)/shard_map/ppermute | solution.py:393
  131.2 0.9 collective-permute-done.2
  132.1 9.0 %all_to_all.67 = f32[4,136,128]{2,1,0:T(8,128)S(1)} all-to-all(f32[4,136,128]{2,1,0:T(8,128)S(1)} %broadcast_in_dim.14), channel_id=1, replica_groups=mesh['zl'=8,'y'=4,'zh'=2,'x'=4,'c'=2] {'x'}, dimensions={0} | all-to-all | bytes 557056 | tf_op jit(solution)/shard_map/all_to_all | solution.py:389
  141.1 7.9 %collective-permute-start.3 = (f32[136,128]{1,0:T(8,128)S(1)}, f32[136,128]{1,0:T(8,128)S(1)}, u32[]{:S(2)}, u32[]{:S(2)}) collective-permute-start(f32[136,128]{1,0:T(8,128)S(1)} %reduce_sum.19.own_ref), channel_id=1, source_target_pairs={{0,8},{8,0},{1,9},{9,1},{2,10},{10,2},{3,11},{11,3},{4,12},{12,4},... | collective-permute-start | bytes 208904 | tf_op jit(solution)/shard_map/ppermute | solution.py:393
  148.9 2.9 %shard_map.111 = (f32[128,128]{1,0:T(8,128)S(1)}, f32[32,128]{1,0:T(8,128)S(1)}, f32[32,128]{1,0:T(8,128)S(1)}, f32[32,32]{1,0:T(8,128)}) custom-call(f32[32,32]{1,0:T(8,128)S(1)} %get-tuple-element.53.gram_ref, f32[32,32]{1,0:T(8,128)S(1)} %get-tuple-element.49.inverse_ref.older_ref, f32[128,128]{1,0:T(8,128)S(1)} %get-tuple-element.54.y_ref, ...), custom_call_target="tpu_custom_call" | custom-call | flops 1000000000 | bytes 4194304 | tf_op jit(solution)/shard_map/pallas_call | solution.py:195
  151.8 4.6 %collective-permute-done.3.other_ref = f32[136,128]{1,0:T(8,128)S(1)} collective-permute-done((f32[136,128]{1,0:T(8,128)S(1)}, f32[136,128]{1,0:T(8,128)S(1)}, u32[]{:S(2)}, u32[]{:S(2)}) %collective-permute-start.3) | collective-permute-done | bytes 69664 | tf_op jit(solution)/shard_map/ppermute | solution.py:393
  156.4 1.7 shard_map.112
  158.1 9.4 %all_to_all.68.in_ref = f32[4,264,128]{2,1,0:T(8,128)S(1)} all-to-all(f32[4,264,128]{2,1,0:T(8,128)S(1)} %get-tuple-element.56), channel_id=1, replica_groups=mesh['zl'=8,'y'=4,'zh'=2,'x'=4,'c'=2] {'y'}, dimensions={0} | all-to-all | bytes 1081344 | tf_op jit(solution)/shard_map/all_to_all | solution.py:389
  167.5 17.3 %all_to_all.69.in_ref = f32[8,40,128]{2,1,0:T(8,128)S(1)} all-to-all(f32[8,40,128]{2,1,0:T(8,128)S(1)} %shard_map.113), channel_id=1, replica_groups=mesh['zl'=8,'y'=4,'zh'=2,'x'=4,'c'=2] {'zl'}, dimensions={0} | all-to-all | bytes 327680 | tf_op jit(solution)/shard_map/all_to_all | solution.py:389
  184.8 2.7 %shard_map.114 = (f32[32,8,128]{2,1,0:T(8,128)S(1)}, f32[32,128]{1,0:T(8,128)}, f32[32,128]{1,0:T(8,128)S(1)}, f32[32,32]{1,0:T(8,128)S(1)}, f32[32,32]{1,0:T(8,128)}, /*index=5*/f32[32,128]{1,0:T(8,128)S(1)}) custom-call(f32[8,40,128]{2,1,0:T(8,128)S(1)} %all_to_all.69.in_ref, f32[32,32]{1,0:T(8,128)S(1)} %get-tuple-element.57.both_ref, ...), custom_call_target="tpu_custom_call" | custom-call | bytes 4194304 | tf_op jit(solution)/shard_map/pallas_call | solution.py:195
  187.5 13.8 %all_to_all.70.in_ref = f32[32,8,128]{2,1,0:T(8,128)S(1)} all-to-all(f32[32,8,128]{2,1,0:T(8,128)S(1)} %get-tuple-element.62), channel_id=1, replica_groups=mesh['zl'=8,'y'=4,'zh'=2,'x'=4,'c'=2] {'y','x','c'}, dimensions={0} | all-to-all | bytes 262144 | tf_op jit(solution)/shard_map/all_to_all | solution.py:389
  201.4 18.7 %all_to_all.71.in_ref = f32[16,8,128]{2,1,0:T(8,128)S(1)} all-to-all(f32[16,8,128]{2,1,0:T(8,128)S(1)} %shard_map.115), channel_id=1, replica_groups=mesh['zl'=8,'y'=4,'zh'=2,'x'=4,'c'=2] {'zh','zl'}, dimensions={0} | all-to-all | bytes 131072 | tf_op jit(solution)/shard_map/all_to_all | solution.py:389
  (34 shorter events, 4.7 us)
Async XLA Ops:
  1.4 34.3 %copy-start = (s32[4,4,128,128]{3,2,1,0:T(8,128)S(1)}, s32[4,4,128,128]{3,2,1,0:T(8,128)}, u32[]{:S(2)}) copy-start(s32[4,4,128,128]{3,2,1,0:T(8,128)} %param.9) | copy-start | bytes 3145732
  24.7 10.9 %copy-start.1 = (s32[4,4]{1,0:T(4,128)S(1)}, s32[4,4]{1,0:T(4,128)}, u32[]{:S(2)}) copy-start(s32[4,4]{1,0:T(4,128)} %cols_ref.7) | copy-start | bytes 196
  36.6 6.8 %collective-permute-start = (f32[128,128]{1,0:T(8,128)S(1)}, f32[128,128]{1,0:T(8,128)S(1)}, u32[]{:S(2)}, u32[]{:S(2)}) collective-permute-start(f32[128,128]{1,0:T(8,128)S(1)} %get-tuple-element.34), channel_id=1, source_target_pairs={{0,1},{1,0},{2,3},{3,2},{4,5},{5,4},{6,7},{7,6},{8,9},{9,8},{10,11... | collective-permute-start | bytes 196616 | tf_op jit(solution)/shard_map/ppermute | solution.py:393
  53.1 8.1 %copy-start.2 = (s32[32,32]{1,0:T(8,128)S(1)}, s32[32,32]{1,0:T(8,128)}, u32[]{:S(2)}) copy-start(s32[32,32]{1,0:T(8,128)} %gram_ref) | copy-start | bytes 12292
  53.1 8.2 %copy-start.3 = (s32[32,32]{1,0:T(8,128)S(1)}, s32[32,32]{1,0:T(8,128)}, u32[]{:S(2)}) copy-start(s32[32,32]{1,0:T(8,128)} %square_ref) | copy-start | bytes 12292
  53.1 8.2 %copy-start.4 = (s32[32,32]{1,0:T(8,128)S(1)}, s32[32,32]{1,0:T(8,128)}, u32[]{:S(2)}) copy-start(s32[32,32]{1,0:T(8,128)} %inverse_ref) | copy-start | bytes 12292
  53.1 8.2 %copy-start.5 = (s32[32,32]{1,0:T(8,128)S(1)}, s32[32,32]{1,0:T(8,128)}, u32[]{:S(2)}) copy-start(s32[32,32]{1,0:T(8,128)} %older_ref) | copy-start | bytes 12292
  53.1 8.2 %copy-start.6 = (s32[32,128]{1,0:T(8,128)S(1)}, s32[32,128]{1,0:T(8,128)}, u32[]{:S(2)}) copy-start(s32[32,128]{1,0:T(8,128)} %earlier_ref) | copy-start | bytes 49156
  53.1 8.2 %copy-start.7 = (s32[32,128]{1,0:T(8,128)S(1)}, s32[32,128]{1,0:T(8,128)}, u32[]{:S(2)}) copy-start(s32[32,128]{1,0:T(8,128)} %earliest_ref) | copy-start | bytes 49156
  53.1 13.9 %collective-permute-start.1 = (f32[128,128]{1,0:T(8,128)S(1)}, f32[128,128]{1,0:T(8,128)S(1)}, u32[]{:S(2)}, u32[]{:S(2)}) collective-permute-start(f32[128,128]{1,0:T(8,128)S(1)} %reduce_sum.18.own_ref), channel_id=1, source_target_pairs={{0,8},{8,0},{1,9},{9,1},{2,10},{10,2},{3,11},{11,3},{4,12},{12,4},... | collective-permute-start | bytes 196616 | tf_op jit(solution)/shard_map/ppermute | solution.py:393
  118.2 13.8 %collective-permute-start.2 = (f32[136,128]{1,0:T(8,128)S(1)}, f32[136,128]{1,0:T(8,128)S(1)}, u32[]{:S(2)}, u32[]{:S(2)}) collective-permute-start(f32[136,128]{1,0:T(8,128)S(1)} %shard_map.110), channel_id=1, source_target_pairs={{0,1},{1,0},{2,3},{3,2},{4,5},{5,4},{6,7},{7,6},{8,9},{9,8},{10,11... | collective-permute-start | bytes 208904 | tf_op jit(solution)/shard_map/ppermute | solution.py:393
  141.1 15.4 %collective-permute-start.3 = (f32[136,128]{1,0:T(8,128)S(1)}, f32[136,128]{1,0:T(8,128)S(1)}, u32[]{:S(2)}, u32[]{:S(2)}) collective-permute-start(f32[136,128]{1,0:T(8,128)S(1)} %reduce_sum.19.own_ref), channel_id=1, source_target_pairs={{0,8},{8,0},{1,9},{9,1},{2,10},{10,2},{3,11},{11,3},{4,12},{12,4},... | collective-permute-start | bytes 208904 | tf_op jit(solution)/shard_map/ppermute | solution.py:393

commit v5 on v4

--- a/solution.py
+++ b/solution.py
@@ -14,6 +14,7 @@
 TILE = 128
 ROW_Z, ROW_Y = 8, 4
 COL_Z, COL_X, COL_C = 2, 4, 2
+Z_LO = ("z0", "z2", "z1")
 ROWS = ROW_Z * ROW_Y
 AHEAD = 3
 SMALL = 8
@@ -205,7 +206,11 @@
 
 
 def tile_at(t):
-    return lax.rem(t, ROW_Y), lax.div(t, ROW_Y) * BLOCK
+    return lax.rem(t, ROW_Y), place(lax.div(t, ROW_Y)) * BLOCK
+
+
+def place(z):
+    return (z & 1) * 4 + (z >> 1)
 
 
 def forward(cols_ref, block_ref, tiles_ref, out_ref, count, slots):
@@ -236,7 +241,7 @@
             sums_ref[cols_ref[r, s + 1]] += terms[:, TILE:]
     for t in range(ROWS):
         whole = sums_ref[t]
-        y, z = t % ROW_Y, t // ROW_Y
+        y, z = t % ROW_Y, place(t // ROW_Y)
         out_ref[y, z * BLOCK : (z + 1) * BLOCK, :] = fold_two(whole[:BLOCK], whole[BLOCK:])
     packed = pack(modp(gram))
     for y in range(ROW_Y):
@@ -257,27 +262,34 @@
     out_ref[count * BLOCK : count * BLOCK + SMALL, :] = modp(square)
 
 
-def backward_first_kernel(count, slots, cols_ref, own_ref, other_ref, tiles_ref, out_ref, y_ref, sums_ref):
+def over_parts(parts_ref, at):
+    total = parts_ref[0, at, :]
+    for k in range(1, parts_ref.shape[0]):
+        total = total + parts_ref[k, at, :]
+    return modp(total)
+
+
+def backward_first_kernel(count, slots, cols_ref, parts_ref, tiles_ref, out_ref, y_ref, sums_ref):
     projected = []
     for r in range(count):
         at = slice(r * BLOCK, (r + 1) * BLOCK)
-        value = modp(own_ref[at, :] + other_ref[at, :])
+        value = over_parts(parts_ref, at)
         y_ref[at, :] = value
         projected.append(value)
     backward(cols_ref, projected, tiles_ref, sums_ref, out_ref, count, slots)
 
 
 def backward_second_kernel(
-    count, slots, cols_ref, own_ref, other_ref, tiles_ref, gram_ref, inv_y_ref, out_ref, both_ref, sums_ref
+    count, slots, cols_ref, parts_ref, tiles_ref, gram_ref, inv_y_ref, out_ref, both_ref, sums_ref
 ):
     small = slice(count * BLOCK, count * BLOCK + SMALL)
-    square = unpack(modp(own_ref[small, :] + other_ref[small, :]))
+    square = unpack(over_parts(parts_ref, small))
     both = modp(square + gram_ref[...])
     both_ref[...] = both
     projected = []
     for r in range(count):
         at = slice(r * BLOCK, (r + 1) * BLOCK)
-        value = modp(own_ref[at, :] + other_ref[at, :])
+        value = over_parts(parts_ref, at)
         projected.append(modp(value - product(both, inv_y_ref[at, :]) + modulus))
     backward(cols_ref, projected, tiles_ref, sums_ref, out_ref, count, slots)
 
@@ -397,9 +409,8 @@
     return lax.optimization_barrier(arrays)
 
 
-def sum_core_x(partial):
-    pair = partial + flip(partial, "c")
-    return jnp.sum(exchange(jnp.broadcast_to(pair[None], (COL_X, *pair.shape)), "x"), axis=0)
+def spread_x(part):
+    return exchange(jnp.broadcast_to(part[None], (COL_X, *part.shape)), "x")
 
 
 def body(entries, tile_cols, block_now, block_prev, block_prev2, gram_prev, square_prev, inverse_prev, inverse_prev2):
@@ -411,51 +422,55 @@
     small = (BLOCK, BLOCK)
     sums = [pltpu.VMEM((ROWS, 2 * BLOCK, TILE), f32)]
 
-    along_z = exchange(jnp.broadcast_to(current[None], (ROW_Z, *shard)), "zl")
+    along_z = exchange(jnp.broadcast_to(current[None], (ROW_Z, *shard)), Z_LO)
     block = exchange(jnp.broadcast_to(along_z.reshape(1, PART, TILE), (ROW_Y, PART, TILE)), "y")
     partial, tiles = call(
         functools.partial(forward_first_kernel, count, slots),
         [((length, TILE), f32), (stored.shape, bf16)], [tile_cols, block, stored], smem=(0,),
     )
-    own = sum_core_x(partial)
-    other = flip(own, "zh")
-    own, *given = together(
-        own, gram_prev, square_prev, inverse_prev, inverse_prev2, current, block_prev, block_prev2
+    other = flip(partial, "zh")
+    partial, *given = together(
+        partial, gram_prev, square_prev, inverse_prev, inverse_prev2, current, block_prev, block_prev2
     )
     base, inverse_old, earlier = call(
         third_kernel, [(shard, f32), (small, f32), (shard, f32)], given, flops=10**9
     )
     other, base, inverse_old, earlier = together(other, base, inverse_old, earlier)
+    pair = partial + other
+    parts = spread_x(pair + flip(pair, "c"))
 
     spread, projected = call(
         functools.partial(backward_first_kernel, count, slots),
         [((ROW_Y, PART + SMALL, TILE), f32), ((length, TILE), f32)],
-        [tile_cols, own, other, tiles], smem=(0,), scratch=sums,
+        [tile_cols, parts, tiles], smem=(0,), scratch=sums,
     )
     chunks = (ROW_Z, BLOCK + SMALL, TILE)
     [by_z] = call(sum_y_kernel, [(chunks, f32)], [exchange(spread, "y")])
     out, shifted, gram_now = call(
         shift_kernel, [(chunks, f32), (shard, f32), (small, f32)],
-        [exchange(by_z, "zl"), inverse_old, earlier, base],
-    )
-
-    [spread] = call(spread_y_kernel, [((ROW_Y, PART + SMALL, TILE), f32)], [exchange(out, "zl")])
+        [exchange(by_z, Z_LO), inverse_old, earlier, base],
+    )
+
+    [spread] = call(spread_y_kernel, [((ROW_Y, PART + SMALL, TILE), f32)], [exchange(out, Z_LO)])
     [partial] = call(
         functools.partial(forward_second_kernel, count, slots),
         [((length + SMALL, TILE), f32)], [tile_cols, exchange(spread, "y"), tiles], smem=(0,),
     )
-    own = sum_core_x(partial)
-    other = flip(own, "zh")
+    other = flip(partial, "zh")
+    partial, gram_now = together(partial, gram_now)
     inv_y, inv_x, old, inverse_now = call(
         functools.partial(inverse_kernel, count),
         [((length, TILE), f32), (shard, f32), (shard, f32), (small, f32)],
         [gram_now, inverse_old, projected, current, earlier],
         flops=10**9,
     )
+    other, inv_y, inv_x, old = together(other, inv_y, inv_x, old)
+    pair = partial + other
+    parts = spread_x(pair + flip(pair, "c"))
     spread, both = call(
         functools.partial(backward_second_kernel, count, slots),
         [((ROW_Y, PART + SMALL, TILE), f32), (small, f32)],
-        [tile_cols, own, other, tiles, gram_now, inv_y], smem=(0,), scratch=sums,
+        [tile_cols, parts, tiles, gram_now, inv_y], smem=(0,), scratch=sums,
     )
     [by_z] = call(sum_y_kernel, [(chunks, f32)], [exchange(spread, "y")])
     near = ROW_Y * COL_X * COL_C
@@ -463,16 +478,16 @@
     out, result, base, gram_next, inverse_next, inv_next = call(
         ending_kernel,
         [((near, SMALL, TILE), f32), (shard, f32), (shard, f32), (small, f32), (small, f32), (shard, f32)],
-        [exchange(by_z, "zl"), both, shifted, inv_x, old],
+        [exchange(by_z, Z_LO), both, shifted, inv_x, old],
     )
     [out] = call(relay_kernel, [((far, SMALL, TILE), f32)], [exchange(out, ("y", "x", "c"))])
-    [later] = call(last_kernel, [(shard, f32)], [exchange(out, ("zh", "zl")), gram_next, base, inv_next])
+    [later] = call(last_kernel, [(shard, f32)], [exchange(out, ("zh", *Z_LO)), gram_next, base, inv_next])
     return result, later
 
 
 def solution(mesh):
-    fine = Mesh(mesh.devices.reshape(ROW_Z, ROW_Y, COL_Z, COL_X, COL_C), ("zl", "y", "zh", "x", "c"))
-    row, col = ("zl", "y"), ("zh", "x", "c")
+    fine = Mesh(mesh.devices.reshape(2, 2, 2, ROW_Y, COL_Z, COL_X, COL_C), ("z2", "z1", "z0", "y", "zh", "x", "c"))
+    row, col = ("z2", "z1", "z0", "y"), ("zh", "x", "c")
     columns = P(None, (*col, *row))
     return jax.shard_map(
         body,

time: 222 us -> 217 us (0.977)
  starting transfers between devices: 34.8 us -> 31.3 us
    ppermute x4, starting transfers between devices: 34.8 us -> 31.3 us  [flip(): return lax.ppermute(x, axis, [(0, 1), (1, 0)])]
where the time goes in v5:
time: 217 us; the launch traced here: 216 us
  blocking collectives  160 us (74%)
  starting transfers between devices  31.3 us (14%)
  Pallas kernels  12.4 us (6%)
  waiting for transfers between devices  10.8 us (5%)
    all_to_all x12, blocking collectives, exchange(): return lax.all_to_all(parts, axis, 0, 0, tiled=True)  160 us
    ppermute x4, starting transfers between devices, flip(): return lax.ppermute(x, axis, [(0, 1), (1, 0)])  31.3 us
    pallas_call x13, Pallas kernels, call(): pl.pallas_call(kernel, out_shape=shapes, in_specs=specs, out_specs=[pl.Bl...  12.4 us
    ppermute x4, waiting for transfers between devices, flip(): return lax.ppermute(x, axis, [(0, 1), (1, 0)])  10.8 us
  transfers between devices with their start and end apart: 4, of which 4 were waited for; matrix products, arithmetic and copies ran while one was open for 0% of the time, Pallas kernels for 2%

profile of v5, /device:TPU:1, one launch (start us, length us, event | category | flops | bytes accessed | tf_op | source)
XLA Modules:
  0.0 215.9 jit_solution(11125623307399726636)
XLA Ops:
  1.4 23.4 %all_to_all.60 = f32[8,32,128]{2,1,0:T(8,128)S(1)} all-to-all(f32[8,32,128]{2,1,0:T(8,128)S(1)} %broadcast_in_dim.10), channel_id=1, replica_groups=mesh['z2'=2,'z1'=2,'z0'=2,'y'=4,'zh'=2,'x'=4,'c'=2] {'z0','z2','z1'}, dimensions={0} | all-to-all | bytes 262144 | tf_op jit(solution)/shard_map/all_to_all | solution.py:401
  24.8 10.9 %all_to_all.61.block_ref = f32[4,256,128]{2,1,0:T(8,128)S(1)} all-to-all(f32[4,256,128]{2,1,0:T(8,128)S(1)} %broadcast_in_dim.12), channel_id=1, replica_groups=mesh['z2'=2,'z1'=2,'z0'=2,'y'=4,'zh'=2,'x'=4,'c'=2] {'y'}, dimensions={0} | all-to-all | bytes 1048576 | tf_op jit(solution)/shard_map/all_to_all | solution.py:401
  35.8 0.9 shard_map.104
  36.7 7.9 %collective-permute-start = (f32[128,128]{1,0:T(8,128)S(1)}, f32[128,128]{1,0:T(8,128)S(1)}, u32[]{:S(2)}, u32[]{:S(2)}) collective-permute-start(f32[128,128]{1,0:T(8,128)S(1)} %get-tuple-element.41), channel_id=1, source_target_pairs={{0,8},{8,0},{1,9},{9,1},{2,10},{10,2},{3,11},{11,3},{4,12},{12,4},... | collective-permute-start | bytes 196616 | tf_op jit(solution)/shard_map/ppermute | solution.py:405
  45.3 5.1 %collective-permute-done = f32[128,128]{1,0:T(8,128)S(1)} collective-permute-done((f32[128,128]{1,0:T(8,128)S(1)}, f32[128,128]{1,0:T(8,128)S(1)}, u32[]{:S(2)}, u32[]{:S(2)}) %collective-permute-start) | collective-permute-done | bytes 65568 | tf_op jit(solution)/shard_map/ppermute | solution.py:405
  50.5 7.7 %collective-permute-start.1 = (f32[128,128]{1,0:T(8,128)S(1)}, f32[128,128]{1,0:T(8,128)S(1)}, u32[]{:S(2)}, u32[]{:S(2)}) collective-permute-start(f32[128,128]{1,0:T(8,128)S(1)} %add.12), channel_id=1, source_target_pairs={{0,1},{1,0},{2,3},{3,2},{4,5},{5,4},{6,7},{7,6},{8,9},{9,8},{10,11... | collective-permute-start | bytes 196616 | tf_op jit(solution)/shard_map/ppermute | solution.py:405
  59.1 9.6 %all_to_all.62.parts_ref = f32[4,128,128]{2,1,0:T(8,128)S(1)} all-to-all(f32[4,128,128]{2,1,0:T(8,128)S(1)} %broadcast_in_dim.13), channel_id=1, replica_groups=mesh['z2'=2,'z1'=2,'z0'=2,'y'=4,'zh'=2,'x'=4,'c'=2] {'x'}, dimensions={0} | all-to-all | bytes 524288 | tf_op jit(solution)/shard_map/all_to_all | solution.py:401
  68.8 1.4 shard_map.106
  70.1 10.3 %all_to_all.63.in_ref = f32[4,264,128]{2,1,0:T(8,128)S(1)} all-to-all(f32[4,264,128]{2,1,0:T(8,128)S(1)} %get-tuple-element.54), channel_id=1, replica_groups=mesh['z2'=2,'z1'=2,'z0'=2,'y'=4,'zh'=2,'x'=4,'c'=2] {'y'}, dimensions={0} | all-to-all | bytes 1081344 | tf_op jit(solution)/shard_map/all_to_all | solution.py:401
  80.4 14.4 %all_to_all.64.in_ref = f32[8,40,128]{2,1,0:T(8,128)S(1)} all-to-all(f32[8,40,128]{2,1,0:T(8,128)S(1)} %shard_map.107), channel_id=1, replica_groups=mesh['z2'=2,'z1'=2,'z0'=2,'y'=4,'zh'=2,'x'=4,'c'=2] {'z0','z2','z1'}, dimensions={0} | all-to-all | bytes 327680 | tf_op jit(solution)/shard_map/all_to_all | solution.py:401
  95.2 14.6 %all_to_all.65.in_ref = f32[8,40,128]{2,1,0:T(8,128)S(1)} all-to-all(f32[8,40,128]{2,1,0:T(8,128)S(1)} %get-tuple-element.58), channel_id=1, replica_groups=mesh['z2'=2,'z1'=2,'z0'=2,'y'=4,'zh'=2,'x'=4,'c'=2] {'z0','z2','z1'}, dimensions={0} | all-to-all | bytes 327680 | tf_op jit(solution)/shard_map/all_to_all | solution.py:401
  109.8 9.4 %all_to_all.66.block_ref = f32[4,264,128]{2,1,0:T(8,128)S(1)} all-to-all(f32[4,264,128]{2,1,0:T(8,128)S(1)} %shard_map.109), channel_id=1, replica_groups=mesh['z2'=2,'z1'=2,'z0'=2,'y'=4,'zh'=2,'x'=4,'c'=2] {'y'}, dimensions={0} | all-to-all | bytes 1081344 | tf_op jit(solution)/shard_map/all_to_all | solution.py:401
  120.1 8.2 %collective-permute-start.2 = (f32[136,128]{1,0:T(8,128)S(1)}, f32[136,128]{1,0:T(8,128)S(1)}, u32[]{:S(2)}, u32[]{:S(2)}) collective-permute-start(f32[136,128]{1,0:T(8,128)S(1)} %shard_map.110), channel_id=1, source_target_pairs={{0,8},{8,0},{1,9},{9,1},{2,10},{10,2},{3,11},{11,3},{4,12},{12,4},... | collective-permute-start | bytes 208904 | tf_op jit(solution)/shard_map/ppermute | solution.py:405
  128.2 2.9 %shard_map.111 = (f32[128,128]{1,0:T(8,128)S(1)}, f32[32,128]{1,0:T(8,128)S(1)}, f32[32,128]{1,0:T(8,128)S(1)}, f32[32,32]{1,0:T(8,128)}) custom-call(f32[32,32]{1,0:T(8,128)S(1)} %get-tuple-element.61.gram_ref, f32[32,32]{1,0:T(8,128)S(1)} %get-tuple-element.55.inverse_ref.older_ref, f32[128,128]{1,0:T(8,128)S(1)} %get-tuple-element.62.y_ref, ...), custom_call_target="tpu_custom_call" | custom-call | flops 1000000000 | bytes 4194304 | tf_op jit(solution)/shard_map/pallas_call | solution.py:196
  131.1 3.9 %collective-permute-done.2 = f32[136,128]{1,0:T(8,128)S(1)} collective-permute-done((f32[136,128]{1,0:T(8,128)S(1)}, f32[136,128]{1,0:T(8,128)S(1)}, u32[]{:S(2)}, u32[]{:S(2)}) %collective-permute-start.2) | collective-permute-done | bytes 69664 | tf_op jit(solution)/shard_map/ppermute | solution.py:405
  135.0 7.5 %collective-permute-start.3 = (f32[136,128]{1,0:T(8,128)S(1)}, f32[136,128]{1,0:T(8,128)S(1)}, u32[]{:S(2)}, u32[]{:S(2)}) collective-permute-start(f32[136,128]{1,0:T(8,128)S(1)} %add.14), channel_id=1, source_target_pairs={{0,1},{1,0},{2,3},{3,2},{4,5},{5,4},{6,7},{7,6},{8,9},{9,8},{10,11... | collective-permute-start | bytes 208904 | tf_op jit(solution)/shard_map/ppermute | solution.py:405
  142.5 0.9 collective-permute-done.3
  143.4 9.0 %all_to_all.67.parts_ref = f32[4,136,128]{2,1,0:T(8,128)S(1)} all-to-all(f32[4,136,128]{2,1,0:T(8,128)S(1)} %broadcast_in_dim.14), channel_id=1, replica_groups=mesh['z2'=2,'z1'=2,'z0'=2,'y'=4,'zh'=2,'x'=4,'c'=2] {'x'}, dimensions={0} | all-to-all | bytes 557056 | tf_op jit(solution)/shard_map/all_to_all | solution.py:401
  152.4 1.7 shard_map.112
  154.0 10.9 %all_to_all.68.in_ref = f32[4,264,128]{2,1,0:T(8,128)S(1)} all-to-all(f32[4,264,128]{2,1,0:T(8,128)S(1)} %get-tuple-element.68), channel_id=1, replica_groups=mesh['z2'=2,'z1'=2,'z0'=2,'y'=4,'zh'=2,'x'=4,'c'=2] {'y'}, dimensions={0} | all-to-all | bytes 1081344 | tf_op jit(solution)/shard_map/all_to_all | solution.py:401
  164.9 13.6 %all_to_all.69.in_ref = f32[8,40,128]{2,1,0:T(8,128)S(1)} all-to-all(f32[8,40,128]{2,1,0:T(8,128)S(1)} %shard_map.113), channel_id=1, replica_groups=mesh['z2'=2,'z1'=2,'z0'=2,'y'=4,'zh'=2,'x'=4,'c'=2] {'z0','z2','z1'}, dimensions={0} | all-to-all | bytes 327680 | tf_op jit(solution)/shard_map/all_to_all | solution.py:401
  178.6 2.7 %shard_map.114 = (f32[32,8,128]{2,1,0:T(8,128)S(1)}, f32[32,128]{1,0:T(8,128)}, f32[32,128]{1,0:T(8,128)S(1)}, f32[32,32]{1,0:T(8,128)S(1)}, f32[32,32]{1,0:T(8,128)}, /*index=5*/f32[32,128]{1,0:T(8,128)S(1)}) custom-call(f32[8,40,128]{2,1,0:T(8,128)S(1)} %all_to_all.69.in_ref, f32[32,32]{1,0:T(8,128)S(1)} %get-tuple-element.69.both_ref, ...), custom_call_target="tpu_custom_call" | custom-call | bytes 4194304 | tf_op jit(solution)/shard_map/pallas_call | solution.py:196
  181.2 14.5 %all_to_all.70.in_ref = f32[32,8,128]{2,1,0:T(8,128)S(1)} all-to-all(f32[32,8,128]{2,1,0:T(8,128)S(1)} %get-tuple-element.74), channel_id=1, replica_groups=mesh['z2'=2,'z1'=2,'z0'=2,'y'=4,'zh'=2,'x'=4,'c'=2] {'y','x','c'}, dimensions={0} | all-to-all | bytes 262144 | tf_op jit(solution)/shard_map/all_to_all | solution.py:401
  195.8 19.2 %all_to_all.71.in_ref = f32[16,8,128]{2,1,0:T(8,128)S(1)} all-to-all(f32[16,8,128]{2,1,0:T(8,128)S(1)} %shard_map.115), channel_id=1, replica_groups=mesh['z2'=2,'z1'=2,'z0'=2,'y'=4,'zh'=2,'x'=4,'c'=2] {'zh','z0','z2','z1'}, dimensions={0} | all-to-all | bytes 131072 | tf_op jit(solution)/shard_map/all_to_all | solution.py:401
  (34 shorter events, 4.7 us)
Async XLA Ops:
  1.4 34.4 %copy-start = (s32[4,4,128,128]{3,2,1,0:T(8,128)S(1)}, s32[4,4,128,128]{3,2,1,0:T(8,128)}, u32[]{:S(2)}) copy-start(s32[4,4,128,128]{3,2,1,0:T(8,128)} %param.9) | copy-start | bytes 3145732
  24.8 10.9 %copy-start.1 = (s32[4,4]{1,0:T(4,128)S(1)}, s32[4,4]{1,0:T(4,128)}, u32[]{:S(2)}) copy-start(s32[4,4]{1,0:T(4,128)} %cols_ref.7) | copy-start | bytes 196
  35.7 8.9 %copy-start.2 = (s32[32,32]{1,0:T(8,128)S(1)}, s32[32,32]{1,0:T(8,128)}, u32[]{:S(2)}) copy-start(s32[32,32]{1,0:T(8,128)} %gram_ref) | copy-start | bytes 12292
  35.7 8.9 %copy-start.3 = (s32[32,32]{1,0:T(8,128)S(1)}, s32[32,32]{1,0:T(8,128)}, u32[]{:S(2)}) copy-start(s32[32,32]{1,0:T(8,128)} %square_ref) | copy-start | bytes 12292
  35.7 8.9 %copy-start.4 = (s32[32,32]{1,0:T(8,128)S(1)}, s32[32,32]{1,0:T(8,128)}, u32[]{:S(2)}) copy-start(s32[32,32]{1,0:T(8,128)} %inverse_ref) | copy-start | bytes 12292
  35.7 8.9 %copy-start.5 = (s32[32,32]{1,0:T(8,128)S(1)}, s32[32,32]{1,0:T(8,128)}, u32[]{:S(2)}) copy-start(s32[32,32]{1,0:T(8,128)} %older_ref) | copy-start | bytes 12292
  35.8 8.9 %copy-start.6 = (s32[32,128]{1,0:T(8,128)S(1)}, s32[32,128]{1,0:T(8,128)}, u32[]{:S(2)}) copy-start(s32[32,128]{1,0:T(8,128)} %earlier_ref) | copy-start | bytes 49156
  35.8 8.9 %copy-start.7 = (s32[32,128]{1,0:T(8,128)S(1)}, s32[32,128]{1,0:T(8,128)}, u32[]{:S(2)}) copy-start(s32[32,128]{1,0:T(8,128)} %earliest_ref) | copy-start | bytes 49156
  36.7 13.8 %collective-permute-start = (f32[128,128]{1,0:T(8,128)S(1)}, f32[128,128]{1,0:T(8,128)S(1)}, u32[]{:S(2)}, u32[]{:S(2)}) collective-permute-start(f32[128,128]{1,0:T(8,128)S(1)} %get-tuple-element.41), channel_id=1, source_target_pairs={{0,8},{8,0},{1,9},{9,1},{2,10},{10,2},{3,11},{11,3},{4,12},{12,4},... | collective-permute-start | bytes 196616 | tf_op jit(solution)/shard_map/ppermute | solution.py:405
  50.5 8.6 %collective-permute-start.1 = (f32[128,128]{1,0:T(8,128)S(1)}, f32[128,128]{1,0:T(8,128)S(1)}, u32[]{:S(2)}, u32[]{:S(2)}) collective-permute-start(f32[128,128]{1,0:T(8,128)S(1)} %add.12), channel_id=1, source_target_pairs={{0,1},{1,0},{2,3},{3,2},{4,5},{5,4},{6,7},{7,6},{8,9},{9,8},{10,11... | collective-permute-start | bytes 196616 | tf_op jit(solution)/shard_map/ppermute | solution.py:405
  120.1 14.9 %collective-permute-start.2 = (f32[136,128]{1,0:T(8,128)S(1)}, f32[136,128]{1,0:T(8,128)S(1)}, u32[]{:S(2)}, u32[]{:S(2)}) collective-permute-start(f32[136,128]{1,0:T(8,128)S(1)} %shard_map.110), channel_id=1, source_target_pairs={{0,8},{8,0},{1,9},{9,1},{2,10},{10,2},{3,11},{11,3},{4,12},{12,4},... | collective-permute-start | bytes 208904 | tf_op jit(solution)/shard_map/ppermute | solution.py:405
  135.0 8.4 %collective-permute-start.3 = (f32[136,128]{1,0:T(8,128)S(1)}, f32[136,128]{1,0:T(8,128)S(1)}, u32[]{:S(2)}, u32[]{:S(2)}) collective-permute-start(f32[136,128]{1,0:T(8,128)S(1)} %add.14), channel_id=1, source_target_pairs={{0,1},{1,0},{2,3},{3,2},{4,5},{5,4},{6,7},{7,6},{8,9},{9,8},{10,11... | collective-permute-start | bytes 208904 | tf_op jit(solution)/shard_map/ppermute | solution.py:405

commit v6 on v5

--- a/solution.py
+++ b/solution.py
@@ -206,11 +206,15 @@
 
 
 def tile_at(t):
-    return lax.rem(t, ROW_Y), place(lax.div(t, ROW_Y)) * BLOCK
+    return across(lax.rem(t, ROW_Y)), place(lax.div(t, ROW_Y)) * BLOCK
 
 
 def place(z):
     return (z & 1) * 4 + (z >> 1)
+
+
+def across(y):
+    return (y & 1) * 2 + (y >> 1)
 
 
 def forward(cols_ref, block_ref, tiles_ref, out_ref, count, slots):
@@ -241,7 +245,7 @@
             sums_ref[cols_ref[r, s + 1]] += terms[:, TILE:]
     for t in range(ROWS):
         whole = sums_ref[t]
-        y, z = t % ROW_Y, place(t // ROW_Y)
+        y, z = across(t % ROW_Y), place(t // ROW_Y)
         out_ref[y, z * BLOCK : (z + 1) * BLOCK, :] = fold_two(whole[:BLOCK], whole[BLOCK:])
     packed = pack(modp(gram))
     for y in range(ROW_Y):
@@ -410,7 +414,7 @@
 
 
 def spread_x(part):
-    return exchange(jnp.broadcast_to(part[None], (COL_X, *part.shape)), "x")
+    return exchange(jnp.broadcast_to(part[None], (COL_X, *part.shape)), ("x0", "x1"))
 
 
 def body(entries, tile_cols, block_now, block_prev, block_prev2, gram_prev, square_prev, inverse_prev, inverse_prev2):
@@ -423,7 +427,7 @@
     sums = [pltpu.VMEM((ROWS, 2 * BLOCK, TILE), f32)]
 
     along_z = exchange(jnp.broadcast_to(current[None], (ROW_Z, *shard)), Z_LO)
-    block = exchange(jnp.broadcast_to(along_z.reshape(1, PART, TILE), (ROW_Y, PART, TILE)), "y")
+    block = exchange(jnp.broadcast_to(along_z.reshape(1, PART, TILE), (ROW_Y, PART, TILE)), ("y0", "y1"))
     partial, tiles = call(
         functools.partial(forward_first_kernel, count, slots),
         [((length, TILE), f32), (stored.shape, bf16)], [tile_cols, block, stored], smem=(0,),
@@ -445,7 +449,7 @@
         [tile_cols, parts, tiles], smem=(0,), scratch=sums,
     )
     chunks = (ROW_Z, BLOCK + SMALL, TILE)
-    [by_z] = call(sum_y_kernel, [(chunks, f32)], [exchange(spread, "y")])
+    [by_z] = call(sum_y_kernel, [(chunks, f32)], [exchange(spread, ("y0", "y1"))])
     out, shifted, gram_now = call(
         shift_kernel, [(chunks, f32), (shard, f32), (small, f32)],
         [exchange(by_z, Z_LO), inverse_old, earlier, base],
@@ -454,7 +458,7 @@
     [spread] = call(spread_y_kernel, [((ROW_Y, PART + SMALL, TILE), f32)], [exchange(out, Z_LO)])
     [partial] = call(
         functools.partial(forward_second_kernel, count, slots),
-        [((length + SMALL, TILE), f32)], [tile_cols, exchange(spread, "y"), tiles], smem=(0,),
+        [((length + SMALL, TILE), f32)], [tile_cols, exchange(spread, ("y0", "y1")), tiles], smem=(0,),
     )
     other = flip(partial, "zh")
     partial, gram_now = together(partial, gram_now)
@@ -472,7 +476,7 @@
         [((ROW_Y, PART + SMALL, TILE), f32), (small, f32)],
         [tile_cols, parts, tiles, gram_now, inv_y], smem=(0,), scratch=sums,
     )
-    [by_z] = call(sum_y_kernel, [(chunks, f32)], [exchange(spread, "y")])
+    [by_z] = call(sum_y_kernel, [(chunks, f32)], [exchange(spread, ("y0", "y1"))])
     near = ROW_Y * COL_X * COL_C
     far = COL_Z * ROW_Z
     out, result, base, gram_next, inverse_next, inv_next = call(
@@ -480,14 +484,14 @@
         [((near, SMALL, TILE), f32), (shard, f32), (shard, f32), (small, f32), (small, f32), (shard, f32)],
         [exchange(by_z, Z_LO), both, shifted, inv_x, old],
     )
-    [out] = call(relay_kernel, [((far, SMALL, TILE), f32)], [exchange(out, ("y", "x", "c"))])
+    [out] = call(relay_kernel, [((far, SMALL, TILE), f32)], [exchange(out, ("y0", "y1", "x0", "x1", "c"))])
     [later] = call(last_kernel, [(shard, f32)], [exchange(out, ("zh", *Z_LO)), gram_next, base, inv_next])
     return result, later
 
 
 def solution(mesh):
-    fine = Mesh(mesh.devices.reshape(2, 2, 2, ROW_Y, COL_Z, COL_X, COL_C), ("z2", "z1", "z0", "y", "zh", "x", "c"))
-    row, col = ("z2", "z1", "z0", "y"), ("zh", "x", "c")
+    fine = Mesh(mesh.devices.reshape(2, 2, 2, 2, 2, COL_Z, 2, 2, COL_C), ("z2", "z1", "z0", "y1", "y0", "zh", "x1", "x0", "c"))
+    row, col = ("z2", "z1", "z0", "y1", "y0"), ("zh", "x1", "x0", "c")
     columns = P(None, (*col, *row))
     return jax.shard_map(
         body,

time: 217 us -> 215 us (level)
  blocking collectives: 160 us -> 156 us
  starting transfers between devices: 31.3 us -> 34 us
    all_to_all x12, blocking collectives: 160 us -> 156 us  [exchange(): return lax.all_to_all(parts, axis, 0, 0, tiled=True)]
    ppermute x4, starting transfers between devices: 31.3 us -> 34 us  [flip(): return lax.ppermute(x, axis, [(0, 1), (1, 0)])]
where the time goes in v6:
time: 215 us
  blocking collectives  156 us (73%)
  starting transfers between devices  34 us (16%)
  Pallas kernels  12.4 us (6%)
  waiting for transfers between devices  10.4 us (5%)
    all_to_all x12, blocking collectives, exchange(): return lax.all_to_all(parts, axis, 0, 0, tiled=True)  156 us
    ppermute x4, starting transfers between devices, flip(): return lax.ppermute(x, axis, [(0, 1), (1, 0)])  34 us
    pallas_call x13, Pallas kernels, call(): pl.pallas_call(kernel, out_shape=shapes, in_specs=specs, out_specs=[pl.Bl...  12.4 us
    ppermute x4, waiting for transfers between devices, flip(): return lax.ppermute(x, axis, [(0, 1), (1, 0)])  10.4 us
  transfers between devices with their start and end apart: 4, of which 4 were waited for; matrix products, arithmetic and copies ran while one was open for 0% of the time, Pallas kernels for 2%

profile of v6, /device:TPU:1, one launch (start us, length us, event | category | flops | bytes accessed | tf_op | source)
XLA Modules:
  0.0 214.6 jit_solution(9163940514384468420)
XLA Ops:
  1.4 23.4 %all_to_all.60 = f32[8,32,128]{2,1,0:T(8,128)S(1)} all-to-all(f32[8,32,128]{2,1,0:T(8,128)S(1)} %broadcast_in_dim.10), channel_id=1, replica_groups=mesh['z2'=2,'z1'=2,'z0'=2,'y1'=2,'y0'=2,'zh'=2,'x1'=2,'x0'=2,'c'=2] {'z0..., dimensions={0} | all-to-all | bytes 262144 | tf_op jit(solution)/shard_map/all_to_all | solution.py:405
  24.8 10.6 %all_to_all.61.block_ref = f32[4,256,128]{2,1,0:T(8,128)S(1)} all-to-all(f32[4,256,128]{2,1,0:T(8,128)S(1)} %broadcast_in_dim.12), channel_id=1, replica_groups=mesh['z2'=2,'z1'=2,'z0'=2,'y1'=2,'y0'=2,'zh'=2,'x1'=2,'x0'=2,'c'=2] {'y0..., dimensions={0} | all-to-all | bytes 1048576 | tf_op jit(solution)/shard_map/all_to_all | solution.py:405
  35.5 0.9 shard_map.104
  36.4 7.9 %collective-permute-start = (f32[128,128]{1,0:T(8,128)S(1)}, f32[128,128]{1,0:T(8,128)S(1)}, u32[]{:S(2)}, u32[]{:S(2)}) collective-permute-start(f32[128,128]{1,0:T(8,128)S(1)} %get-tuple-element.41), channel_id=1, source_target_pairs={{0,8},{8,0},{1,9},{9,1},{2,10},{10,2},{3,11},{11,3},{4,12},{12,4},... | collective-permute-start | bytes 196616 | tf_op jit(solution)/shard_map/ppermute | solution.py:409
  45.0 5.1 %collective-permute-done = f32[128,128]{1,0:T(8,128)S(1)} collective-permute-done((f32[128,128]{1,0:T(8,128)S(1)}, f32[128,128]{1,0:T(8,128)S(1)}, u32[]{:S(2)}, u32[]{:S(2)}) %collective-permute-start) | collective-permute-done | bytes 65568 | tf_op jit(solution)/shard_map/ppermute | solution.py:409
  50.2 7.7 %collective-permute-start.1 = (f32[128,128]{1,0:T(8,128)S(1)}, f32[128,128]{1,0:T(8,128)S(1)}, u32[]{:S(2)}, u32[]{:S(2)}) collective-permute-start(f32[128,128]{1,0:T(8,128)S(1)} %add.12), channel_id=1, source_target_pairs={{0,1},{1,0},{2,3},{3,2},{4,5},{5,4},{6,7},{7,6},{8,9},{9,8},{10,11... | collective-permute-start | bytes 196616 | tf_op jit(solution)/shard_map/ppermute | solution.py:409
  58.8 9.4 %all_to_all.62.parts_ref = f32[4,128,128]{2,1,0:T(8,128)S(1)} all-to-all(f32[4,128,128]{2,1,0:T(8,128)S(1)} %broadcast_in_dim.13), channel_id=1, replica_groups=mesh['z2'=2,'z1'=2,'z0'=2,'y1'=2,'y0'=2,'zh'=2,'x1'=2,'x0'=2,'c'=2] {'x0..., dimensions={0} | all-to-all | bytes 524288 | tf_op jit(solution)/shard_map/all_to_all | solution.py:405
  68.2 1.4 shard_map.106
  69.6 10.0 %all_to_all.63.in_ref = f32[4,264,128]{2,1,0:T(8,128)S(1)} all-to-all(f32[4,264,128]{2,1,0:T(8,128)S(1)} %get-tuple-element.54), channel_id=1, replica_groups=mesh['z2'=2,'z1'=2,'z0'=2,'y1'=2,'y0'=2,'zh'=2,'x1'=2,'x0'=2,'c'=2] {'y0..., dimensions={0} | all-to-all | bytes 1081344 | tf_op jit(solution)/shard_map/all_to_all | solution.py:405
  79.6 14.5 %all_to_all.64.in_ref = f32[8,40,128]{2,1,0:T(8,128)S(1)} all-to-all(f32[8,40,128]{2,1,0:T(8,128)S(1)} %shard_map.107), channel_id=1, replica_groups=mesh['z2'=2,'z1'=2,'z0'=2,'y1'=2,'y0'=2,'zh'=2,'x1'=2,'x0'=2,'c'=2] {'z0..., dimensions={0} | all-to-all | bytes 327680 | tf_op jit(solution)/shard_map/all_to_all | solution.py:405
  94.5 13.3 %all_to_all.65.in_ref = f32[8,40,128]{2,1,0:T(8,128)S(1)} all-to-all(f32[8,40,128]{2,1,0:T(8,128)S(1)} %get-tuple-element.58), channel_id=1, replica_groups=mesh['z2'=2,'z1'=2,'z0'=2,'y1'=2,'y0'=2,'zh'=2,'x1'=2,'x0'=2,'c'=2] {'z0..., dimensions={0} | all-to-all | bytes 327680 | tf_op jit(solution)/shard_map/all_to_all | solution.py:405
  107.8 9.3 %all_to_all.66.block_ref = f32[4,264,128]{2,1,0:T(8,128)S(1)} all-to-all(f32[4,264,128]{2,1,0:T(8,128)S(1)} %shard_map.109), channel_id=1, replica_groups=mesh['z2'=2,'z1'=2,'z0'=2,'y1'=2,'y0'=2,'zh'=2,'x1'=2,'x0'=2,'c'=2] {'y0..., dimensions={0} | all-to-all | bytes 1081344 | tf_op jit(solution)/shard_map/all_to_all | solution.py:405
  118.1 9.0 %collective-permute-start.2 = (f32[136,128]{1,0:T(8,128)S(1)}, f32[136,128]{1,0:T(8,128)S(1)}, u32[]{:S(2)}, u32[]{:S(2)}) collective-permute-start(f32[136,128]{1,0:T(8,128)S(1)} %shard_map.110), channel_id=1, source_target_pairs={{0,8},{8,0},{1,9},{9,1},{2,10},{10,2},{3,11},{11,3},{4,12},{12,4},... | collective-permute-start | bytes 208904 | tf_op jit(solution)/shard_map/ppermute | solution.py:409
  127.0 2.9 %shard_map.111 = (f32[128,128]{1,0:T(8,128)S(1)}, f32[32,128]{1,0:T(8,128)S(1)}, f32[32,128]{1,0:T(8,128)S(1)}, f32[32,32]{1,0:T(8,128)}) custom-call(f32[32,32]{1,0:T(8,128)S(1)} %get-tuple-element.61.gram_ref, f32[32,32]{1,0:T(8,128)S(1)} %get-tuple-element.55.inverse_ref.older_ref, f32[128,128]{1,0:T(8,128)S(1)} %get-tuple-element.62.y_ref, ...), custom_call_target="tpu_custom_call" | custom-call | flops 1000000000 | bytes 4194304 | tf_op jit(solution)/shard_map/pallas_call | solution.py:196
  129.9 3.5 %collective-permute-done.2 = f32[136,128]{1,0:T(8,128)S(1)} collective-permute-done((f32[136,128]{1,0:T(8,128)S(1)}, f32[136,128]{1,0:T(8,128)S(1)}, u32[]{:S(2)}, u32[]{:S(2)}) %collective-permute-start.2) | collective-permute-done | bytes 69664 | tf_op jit(solution)/shard_map/ppermute | solution.py:409
  133.4 9.3 %collective-permute-start.3 = (f32[136,128]{1,0:T(8,128)S(1)}, f32[136,128]{1,0:T(8,128)S(1)}, u32[]{:S(2)}, u32[]{:S(2)}) collective-permute-start(f32[136,128]{1,0:T(8,128)S(1)} %add.14), channel_id=1, source_target_pairs={{0,1},{1,0},{2,3},{3,2},{4,5},{5,4},{6,7},{7,6},{8,9},{9,8},{10,11... | collective-permute-start | bytes 208904 | tf_op jit(solution)/shard_map/ppermute | solution.py:409
  142.8 0.9 collective-permute-done.3
  143.7 9.1 %all_to_all.67.parts_ref = f32[4,136,128]{2,1,0:T(8,128)S(1)} all-to-all(f32[4,136,128]{2,1,0:T(8,128)S(1)} %broadcast_in_dim.14), channel_id=1, replica_groups=mesh['z2'=2,'z1'=2,'z0'=2,'y1'=2,'y0'=2,'zh'=2,'x1'=2,'x0'=2,'c'=2] {'x0..., dimensions={0} | all-to-all | bytes 557056 | tf_op jit(solution)/shard_map/all_to_all | solution.py:405
  152.8 1.7 shard_map.112
  154.5 10.4 %all_to_all.68.in_ref = f32[4,264,128]{2,1,0:T(8,128)S(1)} all-to-all(f32[4,264,128]{2,1,0:T(8,128)S(1)} %get-tuple-element.68), channel_id=1, replica_groups=mesh['z2'=2,'z1'=2,'z0'=2,'y1'=2,'y0'=2,'zh'=2,'x1'=2,'x0'=2,'c'=2] {'y0..., dimensions={0} | all-to-all | bytes 1081344 | tf_op jit(solution)/shard_map/all_to_all | solution.py:405
  164.9 13.2 %all_to_all.69.in_ref = f32[8,40,128]{2,1,0:T(8,128)S(1)} all-to-all(f32[8,40,128]{2,1,0:T(8,128)S(1)} %shard_map.113), channel_id=1, replica_groups=mesh['z2'=2,'z1'=2,'z0'=2,'y1'=2,'y0'=2,'zh'=2,'x1'=2,'x0'=2,'c'=2] {'z0..., dimensions={0} | all-to-all | bytes 327680 | tf_op jit(solution)/shard_map/all_to_all | solution.py:405
  178.2 2.7 %shard_map.114 = (f32[32,8,128]{2,1,0:T(8,128)S(1)}, f32[32,128]{1,0:T(8,128)}, f32[32,128]{1,0:T(8,128)S(1)}, f32[32,32]{1,0:T(8,128)S(1)}, f32[32,32]{1,0:T(8,128)}, /*index=5*/f32[32,128]{1,0:T(8,128)S(1)}) custom-call(f32[8,40,128]{2,1,0:T(8,128)S(1)} %all_to_all.69.in_ref, f32[32,32]{1,0:T(8,128)S(1)} %get-tuple-element.69.both_ref, ...), custom_call_target="tpu_custom_call" | custom-call | bytes 4194304 | tf_op jit(solution)/shard_map/pallas_call | solution.py:196
  180.9 14.7 %all_to_all.70.in_ref = f32[32,8,128]{2,1,0:T(8,128)S(1)} all-to-all(f32[32,8,128]{2,1,0:T(8,128)S(1)} %get-tuple-element.74), channel_id=1, replica_groups=mesh['z2'=2,'z1'=2,'z0'=2,'y1'=2,'y0'=2,'zh'=2,'x1'=2,'x0'=2,'c'=2] {'y0..., dimensions={0} | all-to-all | bytes 262144 | tf_op jit(solution)/shard_map/all_to_all | solution.py:405
  195.6 18.1 %all_to_all.71.in_ref = f32[16,8,128]{2,1,0:T(8,128)S(1)} all-to-all(f32[16,8,128]{2,1,0:T(8,128)S(1)} %shard_map.115), channel_id=1, replica_groups=mesh['z2'=2,'z1'=2,'z0'=2,'y1'=2,'y0'=2,'zh'=2,'x1'=2,'x0'=2,'c'=2] {'zh..., dimensions={0} | all-to-all | bytes 131072 | tf_op jit(solution)/shard_map/all_to_all | solution.py:405
  (34 shorter events, 4.7 us)
Async XLA Ops:
  1.4 34.1 %copy-start = (s32[4,4,128,128]{3,2,1,0:T(8,128)S(1)}, s32[4,4,128,128]{3,2,1,0:T(8,128)}, u32[]{:S(2)}) copy-start(s32[4,4,128,128]{3,2,1,0:T(8,128)} %param.9) | copy-start | bytes 3145732
  24.8 10.6 %copy-start.1 = (s32[4,4]{1,0:T(4,128)S(1)}, s32[4,4]{1,0:T(4,128)}, u32[]{:S(2)}) copy-start(s32[4,4]{1,0:T(4,128)} %cols_ref.7) | copy-start | bytes 196
  35.4 8.9 %copy-start.2 = (s32[32,32]{1,0:T(8,128)S(1)}, s32[32,32]{1,0:T(8,128)}, u32[]{:S(2)}) copy-start(s32[32,32]{1,0:T(8,128)} %gram_ref) | copy-start | bytes 12292
  35.4 8.9 %copy-start.3 = (s32[32,32]{1,0:T(8,128)S(1)}, s32[32,32]{1,0:T(8,128)}, u32[]{:S(2)}) copy-start(s32[32,32]{1,0:T(8,128)} %square_ref) | copy-start | bytes 12292
  35.4 8.9 %copy-start.4 = (s32[32,32]{1,0:T(8,128)S(1)}, s32[32,32]{1,0:T(8,128)}, u32[]{:S(2)}) copy-start(s32[32,32]{1,0:T(8,128)} %inverse_ref) | copy-start | bytes 12292
  35.5 8.9 %copy-start.5 = (s32[32,32]{1,0:T(8,128)S(1)}, s32[32,32]{1,0:T(8,128)}, u32[]{:S(2)}) copy-start(s32[32,32]{1,0:T(8,128)} %older_ref) | copy-start | bytes 12292
  35.5 8.9 %copy-start.6 = (s32[32,128]{1,0:T(8,128)S(1)}, s32[32,128]{1,0:T(8,128)}, u32[]{:S(2)}) copy-start(s32[32,128]{1,0:T(8,128)} %earlier_ref) | copy-start | bytes 49156
  35.5 8.9 %copy-start.7 = (s32[32,128]{1,0:T(8,128)S(1)}, s32[32,128]{1,0:T(8,128)}, u32[]{:S(2)}) copy-start(s32[32,128]{1,0:T(8,128)} %earliest_ref) | copy-start | bytes 49156
  36.4 13.8 %collective-permute-start = (f32[128,128]{1,0:T(8,128)S(1)}, f32[128,128]{1,0:T(8,128)S(1)}, u32[]{:S(2)}, u32[]{:S(2)}) collective-permute-start(f32[128,128]{1,0:T(8,128)S(1)} %get-tuple-element.41), channel_id=1, source_target_pairs={{0,8},{8,0},{1,9},{9,1},{2,10},{10,2},{3,11},{11,3},{4,12},{12,4},... | collective-permute-start | bytes 196616 | tf_op jit(solution)/shard_map/ppermute | solution.py:409
  50.2 8.6 %collective-permute-start.1 = (f32[128,128]{1,0:T(8,128)S(1)}, f32[128,128]{1,0:T(8,128)S(1)}, u32[]{:S(2)}, u32[]{:S(2)}) collective-permute-start(f32[128,128]{1,0:T(8,128)S(1)} %add.12), channel_id=1, source_target_pairs={{0,1},{1,0},{2,3},{3,2},{4,5},{5,4},{6,7},{7,6},{8,9},{9,8},{10,11... | collective-permute-start | bytes 196616 | tf_op jit(solution)/shard_map/ppermute | solution.py:409
  118.1 15.4 %collective-permute-start.2 = (f32[136,128]{1,0:T(8,128)S(1)}, f32[136,128]{1,0:T(8,128)S(1)}, u32[]{:S(2)}, u32[]{:S(2)}) collective-permute-start(f32[136,128]{1,0:T(8,128)S(1)} %shard_map.110), channel_id=1, source_target_pairs={{0,8},{8,0},{1,9},{9,1},{2,10},{10,2},{3,11},{11,3},{4,12},{12,4},... | collective-permute-start | bytes 208904 | tf_op jit(solution)/shard_map/ppermute | solution.py:409
  133.4 10.2 %collective-permute-start.3 = (f32[136,128]{1,0:T(8,128)S(1)}, f32[136,128]{1,0:T(8,128)S(1)}, u32[]{:S(2)}, u32[]{:S(2)}) collective-permute-start(f32[136,128]{1,0:T(8,128)S(1)} %add.14), channel_id=1, source_target_pairs={{0,1},{1,0},{2,3},{3,2},{4,5},{5,4},{6,7},{7,6},{8,9},{9,8},{10,11... | collective-permute-start | bytes 208904 | tf_op jit(solution)/shard_map/ppermute | solution.py:409

commit v7 on v6

--- a/solution.py
+++ b/solution.py
@@ -29,6 +29,10 @@
     return jnp.where(rest >= modulus, rest - modulus, rest)
 
 
+def near(x):
+    return x - jnp.floor(x * (1.0 / 65536.0)) * modulus
+
+
 def digits(x):
     top = jnp.floor(x * (1.0 / 256.0))
     return top, x - top * 256.0
@@ -40,11 +44,11 @@
 
 
 def fold_two(top, low):
-    return modp(modp(modp(top) * 256.0) + low)
+    return modp(near(near(top) * 256.0) + low)
 
 
 def fold_three(upper, middle, lower):
-    return modp(modp(upper) * 15.0 + modp(modp(middle) * 256.0) + lower)
+    return modp(near(upper) * 15.0 + near(modp(middle) * 256.0) + lower)
 
 
 def dot(a, b):

time: 215 us -> 215 us (level)
  no operation moved by 1% of the time
where the time goes in v7:
time: 215 us; the launch traced here: 214 us
  blocking collectives  156 us (73%)
  starting transfers between devices  34 us (16%)
  Pallas kernels  12.1 us (6%)
  waiting for transfers between devices  10.4 us (5%)
    all_to_all x12, blocking collectives, exchange(): return lax.all_to_all(parts, axis, 0, 0, tiled=True)  156 us
    ppermute x4, starting transfers between devices, flip(): return lax.ppermute(x, axis, [(0, 1), (1, 0)])  34 us
    pallas_call x13, Pallas kernels, call(): pl.pallas_call(kernel, out_shape=shapes, in_specs=specs, out_specs=[pl.Bl...  12.1 us
    ppermute x4, waiting for transfers between devices, flip(): return lax.ppermute(x, axis, [(0, 1), (1, 0)])  10.4 us
  transfers between devices with their start and end apart: 4, of which 4 were waited for; matrix products, arithmetic and copies ran while one was open for 0% of the time, Pallas kernels for 2%

profile of v7, /device:TPU:1, one launch (start us, length us, event | category | flops | bytes accessed | tf_op | source)
XLA Modules:
  0.0 214.3 jit_solution(1739271363467570093)
XLA Ops:
  1.4 23.4 %all_to_all.60 = f32[8,32,128]{2,1,0:T(8,128)S(1)} all-to-all(f32[8,32,128]{2,1,0:T(8,128)S(1)} %broadcast_in_dim.10), channel_id=1, replica_groups=mesh['z2'=2,'z1'=2,'z0'=2,'y1'=2,'y0'=2,'zh'=2,'x1'=2,'x0'=2,'c'=2] {'z0..., dimensions={0} | all-to-all | bytes 262144 | tf_op jit(solution)/shard_map/all_to_all | solution.py:409
  24.8 10.6 %all_to_all.61.block_ref = f32[4,256,128]{2,1,0:T(8,128)S(1)} all-to-all(f32[4,256,128]{2,1,0:T(8,128)S(1)} %broadcast_in_dim.12), channel_id=1, replica_groups=mesh['z2'=2,'z1'=2,'z0'=2,'y1'=2,'y0'=2,'zh'=2,'x1'=2,'x0'=2,'c'=2] {'y0..., dimensions={0} | all-to-all | bytes 1048576 | tf_op jit(solution)/shard_map/all_to_all | solution.py:409
  35.5 0.9 shard_map.104
  36.4 7.9 %collective-permute-start = (f32[128,128]{1,0:T(8,128)S(1)}, f32[128,128]{1,0:T(8,128)S(1)}, u32[]{:S(2)}, u32[]{:S(2)}) collective-permute-start(f32[128,128]{1,0:T(8,128)S(1)} %get-tuple-element.41), channel_id=1, source_target_pairs={{0,8},{8,0},{1,9},{9,1},{2,10},{10,2},{3,11},{11,3},{4,12},{12,4},... | collective-permute-start | bytes 196616 | tf_op jit(solution)/shard_map/ppermute | solution.py:413
  45.0 5.1 %collective-permute-done = f32[128,128]{1,0:T(8,128)S(1)} collective-permute-done((f32[128,128]{1,0:T(8,128)S(1)}, f32[128,128]{1,0:T(8,128)S(1)}, u32[]{:S(2)}, u32[]{:S(2)}) %collective-permute-start) | collective-permute-done | bytes 65568 | tf_op jit(solution)/shard_map/ppermute | solution.py:413
  50.2 7.7 %collective-permute-start.1 = (f32[128,128]{1,0:T(8,128)S(1)}, f32[128,128]{1,0:T(8,128)S(1)}, u32[]{:S(2)}, u32[]{:S(2)}) collective-permute-start(f32[128,128]{1,0:T(8,128)S(1)} %add.12), channel_id=1, source_target_pairs={{0,1},{1,0},{2,3},{3,2},{4,5},{5,4},{6,7},{7,6},{8,9},{9,8},{10,11... | collective-permute-start | bytes 196616 | tf_op jit(solution)/shard_map/ppermute | solution.py:413
  58.8 9.4 %all_to_all.62.parts_ref = f32[4,128,128]{2,1,0:T(8,128)S(1)} all-to-all(f32[4,128,128]{2,1,0:T(8,128)S(1)} %broadcast_in_dim.13), channel_id=1, replica_groups=mesh['z2'=2,'z1'=2,'z0'=2,'y1'=2,'y0'=2,'zh'=2,'x1'=2,'x0'=2,'c'=2] {'x0..., dimensions={0} | all-to-all | bytes 524288 | tf_op jit(solution)/shard_map/all_to_all | solution.py:409
  68.2 1.3 shard_map.106
  69.5 10.0 %all_to_all.63.in_ref = f32[4,264,128]{2,1,0:T(8,128)S(1)} all-to-all(f32[4,264,128]{2,1,0:T(8,128)S(1)} %get-tuple-element.54), channel_id=1, replica_groups=mesh['z2'=2,'z1'=2,'z0'=2,'y1'=2,'y0'=2,'zh'=2,'x1'=2,'x0'=2,'c'=2] {'y0..., dimensions={0} | all-to-all | bytes 1081344 | tf_op jit(solution)/shard_map/all_to_all | solution.py:409
  79.5 14.5 %all_to_all.64.in_ref = f32[8,40,128]{2,1,0:T(8,128)S(1)} all-to-all(f32[8,40,128]{2,1,0:T(8,128)S(1)} %shard_map.107), channel_id=1, replica_groups=mesh['z2'=2,'z1'=2,'z0'=2,'y1'=2,'y0'=2,'zh'=2,'x1'=2,'x0'=2,'c'=2] {'z0..., dimensions={0} | all-to-all | bytes 327680 | tf_op jit(solution)/shard_map/all_to_all | solution.py:409
  94.4 13.3 %all_to_all.65.in_ref = f32[8,40,128]{2,1,0:T(8,128)S(1)} all-to-all(f32[8,40,128]{2,1,0:T(8,128)S(1)} %get-tuple-element.58), channel_id=1, replica_groups=mesh['z2'=2,'z1'=2,'z0'=2,'y1'=2,'y0'=2,'zh'=2,'x1'=2,'x0'=2,'c'=2] {'z0..., dimensions={0} | all-to-all | bytes 327680 | tf_op jit(solution)/shard_map/all_to_all | solution.py:409
  107.7 9.3 %all_to_all.66.block_ref = f32[4,264,128]{2,1,0:T(8,128)S(1)} all-to-all(f32[4,264,128]{2,1,0:T(8,128)S(1)} %shard_map.109), channel_id=1, replica_groups=mesh['z2'=2,'z1'=2,'z0'=2,'y1'=2,'y0'=2,'zh'=2,'x1'=2,'x0'=2,'c'=2] {'y0..., dimensions={0} | all-to-all | bytes 1081344 | tf_op jit(solution)/shard_map/all_to_all | solution.py:409
  117.9 9.0 %collective-permute-start.2 = (f32[136,128]{1,0:T(8,128)S(1)}, f32[136,128]{1,0:T(8,128)S(1)}, u32[]{:S(2)}, u32[]{:S(2)}) collective-permute-start(f32[136,128]{1,0:T(8,128)S(1)} %shard_map.110), channel_id=1, source_target_pairs={{0,8},{8,0},{1,9},{9,1},{2,10},{10,2},{3,11},{11,3},{4,12},{12,4},... | collective-permute-start | bytes 208904 | tf_op jit(solution)/shard_map/ppermute | solution.py:413
  126.9 2.9 %shard_map.111 = (f32[128,128]{1,0:T(8,128)S(1)}, f32[32,128]{1,0:T(8,128)S(1)}, f32[32,128]{1,0:T(8,128)S(1)}, f32[32,32]{1,0:T(8,128)}) custom-call(f32[32,32]{1,0:T(8,128)S(1)} %get-tuple-element.61.gram_ref, f32[32,32]{1,0:T(8,128)S(1)} %get-tuple-element.55.inverse_ref.older_ref, f32[128,128]{1,0:T(8,128)S(1)} %get-tuple-element.62.y_ref, ...), custom_call_target="tpu_custom_call" | custom-call | flops 1000000000 | bytes 4194304 | tf_op jit(solution)/shard_map/pallas_call | solution.py:200
  129.8 3.5 %collective-permute-done.2 = f32[136,128]{1,0:T(8,128)S(1)} collective-permute-done((f32[136,128]{1,0:T(8,128)S(1)}, f32[136,128]{1,0:T(8,128)S(1)}, u32[]{:S(2)}, u32[]{:S(2)}) %collective-permute-start.2) | collective-permute-done | bytes 69664 | tf_op jit(solution)/shard_map/ppermute | solution.py:413
  133.3 9.3 %collective-permute-start.3 = (f32[136,128]{1,0:T(8,128)S(1)}, f32[136,128]{1,0:T(8,128)S(1)}, u32[]{:S(2)}, u32[]{:S(2)}) collective-permute-start(f32[136,128]{1,0:T(8,128)S(1)} %add.14), channel_id=1, source_target_pairs={{0,1},{1,0},{2,3},{3,2},{4,5},{5,4},{6,7},{7,6},{8,9},{9,8},{10,11... | collective-permute-start | bytes 208904 | tf_op jit(solution)/shard_map/ppermute | solution.py:413
  142.6 0.9 collective-permute-done.3
  143.6 9.2 %all_to_all.67.parts_ref = f32[4,136,128]{2,1,0:T(8,128)S(1)} all-to-all(f32[4,136,128]{2,1,0:T(8,128)S(1)} %broadcast_in_dim.14), channel_id=1, replica_groups=mesh['z2'=2,'z1'=2,'z0'=2,'y1'=2,'y0'=2,'zh'=2,'x1'=2,'x0'=2,'c'=2] {'x0..., dimensions={0} | all-to-all | bytes 557056 | tf_op jit(solution)/shard_map/all_to_all | solution.py:409
  152.7 1.5 shard_map.112
  154.3 10.4 %all_to_all.68.in_ref = f32[4,264,128]{2,1,0:T(8,128)S(1)} all-to-all(f32[4,264,128]{2,1,0:T(8,128)S(1)} %get-tuple-element.68), channel_id=1, replica_groups=mesh['z2'=2,'z1'=2,'z0'=2,'y1'=2,'y0'=2,'zh'=2,'x1'=2,'x0'=2,'c'=2] {'y0..., dimensions={0} | all-to-all | bytes 1081344 | tf_op jit(solution)/shard_map/all_to_all | solution.py:409
  164.7 13.2 %all_to_all.69.in_ref = f32[8,40,128]{2,1,0:T(8,128)S(1)} all-to-all(f32[8,40,128]{2,1,0:T(8,128)S(1)} %shard_map.113), channel_id=1, replica_groups=mesh['z2'=2,'z1'=2,'z0'=2,'y1'=2,'y0'=2,'zh'=2,'x1'=2,'x0'=2,'c'=2] {'z0..., dimensions={0} | all-to-all | bytes 327680 | tf_op jit(solution)/shard_map/all_to_all | solution.py:409
  177.9 2.7 %shard_map.114 = (f32[32,8,128]{2,1,0:T(8,128)S(1)}, f32[32,128]{1,0:T(8,128)}, f32[32,128]{1,0:T(8,128)S(1)}, f32[32,32]{1,0:T(8,128)S(1)}, f32[32,32]{1,0:T(8,128)}, /*index=5*/f32[32,128]{1,0:T(8,128)S(1)}) custom-call(f32[8,40,128]{2,1,0:T(8,128)S(1)} %all_to_all.69.in_ref, f32[32,32]{1,0:T(8,128)S(1)} %get-tuple-element.69.both_ref, ...), custom_call_target="tpu_custom_call" | custom-call | bytes 4194304 | tf_op jit(solution)/shard_map/pallas_call | solution.py:200
  180.6 14.7 %all_to_all.70.in_ref = f32[32,8,128]{2,1,0:T(8,128)S(1)} all-to-all(f32[32,8,128]{2,1,0:T(8,128)S(1)} %get-tuple-element.74), channel_id=1, replica_groups=mesh['z2'=2,'z1'=2,'z0'=2,'y1'=2,'y0'=2,'zh'=2,'x1'=2,'x0'=2,'c'=2] {'y0..., dimensions={0} | all-to-all | bytes 262144 | tf_op jit(solution)/shard_map/all_to_all | solution.py:409
  195.4 18.1 %all_to_all.71.in_ref = f32[16,8,128]{2,1,0:T(8,128)S(1)} all-to-all(f32[16,8,128]{2,1,0:T(8,128)S(1)} %shard_map.115), channel_id=1, replica_groups=mesh['z2'=2,'z1'=2,'z0'=2,'y1'=2,'y0'=2,'zh'=2,'x1'=2,'x0'=2,'c'=2] {'zh..., dimensions={0} | all-to-all | bytes 131072 | tf_op jit(solution)/shard_map/all_to_all | solution.py:409
  (34 shorter events, 4.6 us)
Async XLA Ops:
  1.4 34.1 %copy-start = (s32[4,4,128,128]{3,2,1,0:T(8,128)S(1)}, s32[4,4,128,128]{3,2,1,0:T(8,128)}, u32[]{:S(2)}) copy-start(s32[4,4,128,128]{3,2,1,0:T(8,128)} %param.9) | copy-start | bytes 3145732
  24.8 10.6 %copy-start.1 = (s32[4,4]{1,0:T(4,128)S(1)}, s32[4,4]{1,0:T(4,128)}, u32[]{:S(2)}) copy-start(s32[4,4]{1,0:T(4,128)} %cols_ref.7) | copy-start | bytes 196
  35.4 8.9 %copy-start.2 = (s32[32,32]{1,0:T(8,128)S(1)}, s32[32,32]{1,0:T(8,128)}, u32[]{:S(2)}) copy-start(s32[32,32]{1,0:T(8,128)} %gram_ref) | copy-start | bytes 12292
  35.4 8.9 %copy-start.3 = (s32[32,32]{1,0:T(8,128)S(1)}, s32[32,32]{1,0:T(8,128)}, u32[]{:S(2)}) copy-start(s32[32,32]{1,0:T(8,128)} %square_ref) | copy-start | bytes 12292
  35.4 8.9 %copy-start.4 = (s32[32,32]{1,0:T(8,128)S(1)}, s32[32,32]{1,0:T(8,128)}, u32[]{:S(2)}) copy-start(s32[32,32]{1,0:T(8,128)} %inverse_ref) | copy-start | bytes 12292
  35.5 8.9 %copy-start.5 = (s32[32,32]{1,0:T(8,128)S(1)}, s32[32,32]{1,0:T(8,128)}, u32[]{:S(2)}) copy-start(s32[32,32]{1,0:T(8,128)} %older_ref) | copy-start | bytes 12292
  35.5 8.9 %copy-start.6 = (s32[32,128]{1,0:T(8,128)S(1)}, s32[32,128]{1,0:T(8,128)}, u32[]{:S(2)}) copy-start(s32[32,128]{1,0:T(8,128)} %earlier_ref) | copy-start | bytes 49156
  35.5 8.9 %copy-start.7 = (s32[32,128]{1,0:T(8,128)S(1)}, s32[32,128]{1,0:T(8,128)}, u32[]{:S(2)}) copy-start(s32[32,128]{1,0:T(8,128)} %earliest_ref) | copy-start | bytes 49156
  36.4 13.8 %collective-permute-start = (f32[128,128]{1,0:T(8,128)S(1)}, f32[128,128]{1,0:T(8,128)S(1)}, u32[]{:S(2)}, u32[]{:S(2)}) collective-permute-start(f32[128,128]{1,0:T(8,128)S(1)} %get-tuple-element.41), channel_id=1, source_target_pairs={{0,8},{8,0},{1,9},{9,1},{2,10},{10,2},{3,11},{11,3},{4,12},{12,4},... | collective-permute-start | bytes 196616 | tf_op jit(solution)/shard_map/ppermute | solution.py:413
  50.2 8.6 %collective-permute-start.1 = (f32[128,128]{1,0:T(8,128)S(1)}, f32[128,128]{1,0:T(8,128)S(1)}, u32[]{:S(2)}, u32[]{:S(2)}) collective-permute-start(f32[128,128]{1,0:T(8,128)S(1)} %add.12), channel_id=1, source_target_pairs={{0,1},{1,0},{2,3},{3,2},{4,5},{5,4},{6,7},{7,6},{8,9},{9,8},{10,11... | collective-permute-start | bytes 196616 | tf_op jit(solution)/shard_map/ppermute | solution.py:413
  117.9 15.4 %collective-permute-start.2 = (f32[136,128]{1,0:T(8,128)S(1)}, f32[136,128]{1,0:T(8,128)S(1)}, u32[]{:S(2)}, u32[]{:S(2)}) collective-permute-start(f32[136,128]{1,0:T(8,128)S(1)} %shard_map.110), channel_id=1, source_target_pairs={{0,8},{8,0},{1,9},{9,1},{2,10},{10,2},{3,11},{11,3},{4,12},{12,4},... | collective-permute-start | bytes 208904 | tf_op jit(solution)/shard_map/ppermute | solution.py:413
  133.3 10.2 %collective-permute-start.3 = (f32[136,128]{1,0:T(8,128)S(1)}, f32[136,128]{1,0:T(8,128)S(1)}, u32[]{:S(2)}, u32[]{:S(2)}) collective-permute-start(f32[136,128]{1,0:T(8,128)S(1)} %add.14), channel_id=1, source_target_pairs={{0,1},{1,0},{2,3},{3,2},{4,5},{5,4},{6,7},{7,6},{8,9},{9,8},{10,11... | collective-permute-start | bytes 208904 | tf_op jit(solution)/shard_map/ppermute | solution.py:413
